TPU v7x, 512 devices: a whole 4x8x8 slice. The times are simulated.
512 devices in a mesh: height: 32 (over y_hi, x, core), chan: 16 (over y_lo, z).
Axes of the slice: x: 4, y: 8 (y_hi: 4, y_lo: 2; y = y_hi * 2 + y_lo), z: 8, core: 2. Of those that a mesh axis runs over, the one named last changes fastest.
Arguments:
- saved: int32 [4, 128, 120, 512], P(None, 'height', None, 'chan'), may hold values from -127 to 127
- exponents: int32 [4, 128, 120, 4], P(None, 'height'), may hold values from -14 to -10
- out_grad: bfloat16 [4, 128, 120, 512], P(None, 'height', None, 'chan'), may hold values from -6 to 6
- kernel: bfloat16 [512, 3, 3, 3, 512], P('chan', None, None, None, 'height'), may hold values from -0.0546875 to 0.0546875
Outputs:
- input_grad: bfloat16 [4, 128, 120, 512], P(None, 'height', None, 'chan')
- kernel_grad: float32 [512, 3, 3, 3, 512], P('chan', None, None, None, 'height')
All inputs are finite; a program needn't handle non-finite values.
Results may differ from a plain program's by a relative error of at most 0.001.
Values may be sent and summed in bfloat16 or wider, within the bound.
No kernel may reach another device: no remote copies, remote signals or barrier semaphores. Data moves between devices by JAX's collectives and lax.ppermute only.
A program may use at most 192 MiB of HBM per device.

v0:
```python
import jax
import jax.numpy as jnp
from jax import lax
from jax.sharding import PartitionSpec as P

QB = 128


def padded_2(array, sides, width):
    for axis, dim in sides:
        size, length = (lax.axis_size(axis), array.shape[dim])
        up = [(i, (i + 1) % size) for i in range(size - 1)]
        down = [(j, i) for i, j in up]
        last = lax.slice_in_dim(array, length - width, length, axis=dim)
        initial = lax.slice_in_dim(array, 0, width, axis=dim)
        before = lax.ppermute(last, axis, up)
        after = lax.ppermute(initial, axis, down)
        array = jnp.concatenate([before, array, after], axis=dim)
    return array


def dequant(saved, exponents):
    width = saved.shape[3]
    blocks = max(width // QB, 1)
    first = lax.axis_index("chan") * width // QB
    part = lax.dynamic_slice_in_dim(exponents, first, blocks, 3)
    factor = jnp.repeat(jnp.exp2(part.astype(jnp.float32)), width // blocks, axis=3)
    return (saved.astype(jnp.float32) * factor).astype(jnp.bfloat16)


def pad_piece(piece):
    return jnp.pad(piece, ((0, 2), (0, 0), (1, 1), (0, 0)))


def tap_terms(padded, x_rows, kernel_part):
    frames = padded.shape[0] - 2
    rows_here = padded.shape[1] - 2
    width = padded.shape[2] - 2
    count = padded.shape[3]
    local_ch = x_rows.shape[1]
    row_count = frames * rows_here * width
    total = jnp.zeros((row_count, local_ch), jnp.float32)
    pieces = []
    for frame_tap in range(3):
        for row_tap in range(3):
            for col_tap in range(3):
                shifted = padded[
                    2 - frame_tap : 2 - frame_tap + frames,
                    2 - row_tap : 2 - row_tap + rows_here,
                    2 - col_tap : 2 - col_tap + width,
                ]
                shifted = shifted.reshape(row_count, count)
                total = total + lax.dot_general(
                    shifted,
                    kernel_part[:, frame_tap, row_tap, col_tap, :],
                    (((1,), (1,)), ((), ())),
                    preferred_element_type=jnp.float32,
                )
                pieces.append(
                    lax.dot_general(
                        x_rows,
                        shifted,
                        (((0,), (0,)), ((), ())),
                        preferred_element_type=jnp.float32,
                    )
                )
    return (total, jnp.stack(pieces, axis=1).reshape(local_ch, 3, 3, 3, count))


def local(saved, exponents, out_grad, kernel):
    x_local = dequant(saved, exponents)
    frames, rows_here, width, local_ch = x_local.shape
    row_count = frames * rows_here * width
    x_rows = x_local.reshape(row_count, local_ch)
    kernel_all = lax.all_gather(kernel, "height", axis=4, tiled=True)
    rimmed = padded_2(out_grad, (("height", 1),), 1)
    added, block = tap_terms(
        pad_piece(lax.all_gather(rimmed, "chan", axis=3, tiled=True)), x_rows, kernel_all
    )
    kernel_grad = lax.psum_scatter(block, "height", scatter_dimension=4, tiled=True)
    input_grad = added.reshape(frames, rows_here, width, local_ch).astype(jnp.bfloat16)
    return (input_grad, kernel_grad)


def solution(mesh):
    in_specs = (
        P(None, "height", None, "chan"),
        P(None, "height", None, None),
        P(None, "height", None, "chan"),
        P("chan", None, None, None, "height"),
    )
    out_specs = (P(None, "height", None, "chan"), P("chan", None, None, None, "height"))
    return jax.shard_map(local, mesh=mesh, in_specs=in_specs, out_specs=out_specs, check_vma=False)
```

profile of v0, /device:TPU:1, one launch (start us, length us, event | category | flops | bytes accessed | tf_op | source)
XLA Modules:
  0.0 291.9 jit_solution(10387612414550452817)
XLA Ops:
  7.2 0.8 fusion.33
  8.0 8.8 %collective-permute-start.1 = (bf16[4,1,120,32]{2,3,1,0:T(8,128)(2,1)S(1)}, bf16[4,1,120,32]{2,3,1,0:T(8,128)(2,1)S(1)}, u32[]{:S(2)}, u32[]{:S(2)}) collective-permute-start(bf16[4,1,120,32]{2,3,1,0:T(8,128)(2,1)S(1)} %get-tuple-element.34), channel_id=1, source_target_pairs={{16,0},{32,16},{48,32},{64,48},{80,64},{96,80},{112,96},{128,112},... | collective-permute-start | bytes 92168 | tf_op jit(solution)/shard_map/ppermute | solution.py:17
  16.8 1.9 collective-permute-start
  18.7 1.2 collective-permute-done
  19.9 1.0 pad_maximum_fusion
  20.8 0.8 copy.11
  21.8 0.8 multiply_exponential_fusion
  22.6 1.0 multiply_convert_fusion
  23.5 71.0 %all_gather.7 = bf16[32,3,3,3,512]{0,4,3,2,1:T(8,128)(2,1)} all-gather(bf16[32,3,3,3,16]{0,4,3,2,1:T(8,128)(2,1)} %param.7), channel_id=1, replica_groups=mesh['height'=32,'chan'=16] {'height'}, dimensions={4}, use_global_device_ids=true | all-gather | bytes 912384 | tf_op jit(solution)/shard_map/all_gather | solution.py:75
  94.5 14.1 %all-gather.2.cloned.1.call-done = bf16[4,6,120,512]{2,0,1,3:T(4,128)(2,1)} async-done(((bf16[4,6,120,32]{2,0,1,3:T(4,128)(2,1)}), bf16[4,6,120,512]{2,0,1,3:T(4,128)(2,1)}) %all-gather.2.cloned.1.call-update) | async-done | bytes 2949136 | tf_op jit(solution)/shard_map/all_gather | solution.py:78
  108.7 4.3 %copy.12 = bf16[4,6,120,512]{3,2,1,0:T(8,128)(2,1)S(1)} copy(bf16[4,6,120,512]{2,0,1,3:T(4,128)(2,1)} %all-gather.2.cloned.1.call-done) | data formatting | bytes 5898240 | tf_op jit(solution)/shard_map/all_gather | solution.py:78
  113.0 9.3 %fusion.32 = (bf16[4,4,120,512]{3,2,1,0:T(8,128)(2,1)}, bf16[4,4,120,512]{3,2,1,0:T(8,128)(2,1)}, bf16[4,4,120,512]{3,2,1,0:T(8,128)(2,1)}, bf16[4,4,120,512]{3,...) fusion(bf16[4,6,120,512]{3,2,1,0:T(8,128)(2,1)S(1)} %copy.12), kind=kLoop, calls=%fused_computation.139 | loop fusion | bytes 24576000 | tf_op jit(solution)/shard_map/slice | solution.py:47
  122.3 15.9 %pad_slice_fusion = (bf16[4,4,120,512]{3,2,1,0:T(8,128)(2,1)}, bf16[4,4,120,512]{3,2,1,0:T(8,128)(2,1)}, bf16[4,4,120,512]{3,2,1,0:T(8,128)(2,1)}, bf16[4,4,120,...) fusion(bf16[4,6,120,512]{3,2,1,0:T(8,128)(2,1)S(1)} %copy.12), kind=kLoop, calls=%fused_computation | loop fusion | bytes 40304640 | tf_op jit(solution)/shard_map/slice | solution.py:47
  147.4 0.7 fusion.7
  149.2 0.7 fusion.4
  151.7 1.2 copy-done.27
  152.9 5.3 %copy.16 = f32[32,3,3,3,512]{0,4,3,2,1:T(8,128)} copy(f32[32,3,3,3,512]{4,0,3,2,1:T(8,128)} %bitcast.409) | data formatting | bytes 3538944 | tf_op jit(solution)/shard_map/reshape | solution.py:67
  158.3 2.0 copy-done
  160.2 2.4 fusion.28
  162.6 0.7 convolution_add_fusion.25
  163.3 0.7 convolution_add_fusion.24
  164.2 0.7 convolution_add_fusion.23
  165.0 0.7 convolution_add_fusion.22
  165.8 0.7 convolution_add_fusion.21
  166.7 0.7 convolution_add_fusion.20
  167.5 0.7 convolution_add_fusion.19
  168.4 0.7 convolution_add_fusion.18
  169.2 0.7 convolution_add_fusion.17
  170.1 0.7 convolution_add_fusion.16
  170.9 0.7 convolution_add_fusion.15
  171.8 0.7 convolution_add_fusion.14
  172.6 0.7 convolution_add_fusion.13
  173.5 0.7 convolution_add_fusion.12
  174.3 0.7 convolution_add_fusion.11
  175.2 0.7 convolution_add_fusion.10
  176.0 0.7 convolution_add_fusion.9
  176.9 0.7 convolution_add_fusion.8
  177.7 0.7 convolution_add_fusion.7
  178.7 0.7 convolution_add_fusion.6
  179.4 0.7 convolution_add_fusion.5
  180.4 0.7 convolution_add_fusion.4
  181.1 0.7 convolution_add_fusion.3
  182.1 0.7 convolution_add_fusion.2
  182.9 0.7 convolution_add_fusion.1
  183.9 1.3 fusion
  185.3 1.2 convert_element_type.18
  186.5 0.7 copy.17
  187.2 97.9 %reduce-scatter.2.cloned.1.call-done = f32[32,3,3,3,16]{0,4,3,2,1:T(8,128)} async-done(((f32[32,3,3,3,512]{0,4,3,2,1:T(8,128)}), f32[32,3,3,3,16]{0,4,3,2,1:T(8,128)}) %reduce-scatter.2.cloned.1.call-update) | async-done | bytes 55312 | tf_op jit(solution)/shard_map/reduce_scatter | solution.py:80
  (84 shorter events, 16.0 us)
Async XLA Ops:
  7.2 101.5 %all-gather.2.cloned.1.call-start = ((), (), s32[]{:S(2)}) async-start(), calls=%async_computation.1 | async-start | bytes 3342336 | tf_op jit(solution)/shard_map/all_gather | solution.py:78
  8.0 10.7 %collective-permute-start.1 = (bf16[4,1,120,32]{2,3,1,0:T(8,128)(2,1)S(1)}, bf16[4,1,120,32]{2,3,1,0:T(8,128)(2,1)S(1)}, u32[]{:S(2)}, u32[]{:S(2)}) collective-permute-start(bf16[4,1,120,32]{2,3,1,0:T(8,128)(2,1)S(1)} %get-tuple-element.34), channel_id=1, source_target_pairs={{16,0},{32,16},{48,32},{64,48},{80,64},{96,80},{112,96},{128,112},... | collective-permute-start | bytes 92168 | tf_op jit(solution)/shard_map/ppermute | solution.py:17
  16.8 3.1 %collective-permute-start = (bf16[4,1,120,32]{2,3,1,0:T(8,128)(2,1)S(1)}, bf16[4,1,120,32]{2,3,1,0:T(8,128)(2,1)S(1)}, u32[]{:S(2)}, u32[]{:S(2)}) collective-permute-start(bf16[4,1,120,32]{2,3,1,0:T(8,128)(2,1)S(1)} %get-tuple-element.33), channel_id=1, source_target_pairs={{0,16},{16,32},{32,48},{48,64},{64,80},{80,96},{96,112},{112,128},... | collective-permute-start | bytes 92168 | tf_op jit(solution)/shard_map/ppermute | solution.py:16
  21.7 263.3 %reduce-scatter.2.cloned.1.call-start = ((), (), s32[]{:S(2)}) async-start(), calls=%async_computation.2 | async-start | bytes 7299072 | tf_op jit(solution)/shard_map/reduce_scatter | solution.py:80
  151.7 1.2 copy-start.27
  158.2 2.0 copy-start
  158.2 4.4 %copy-start.26 = (bf16[4,4,120,512]{3,2,1,0:T(8,128)(2,1)S(1)}, bf16[4,4,120,512]{3,2,1,0:T(8,128)(2,1)}, u32[]{:S(2)}) copy-start(bf16[4,4,120,512]{3,2,1,0:T(8,128)(2,1)} %get-tuple-element.7) | copy-start | bytes 5898244
  160.2 3.1 %copy-start.25 = (bf16[4,4,120,512]{3,2,1,0:T(8,128)(2,1)S(1)}, bf16[4,4,120,512]{3,2,1,0:T(8,128)(2,1)}, u32[]{:S(2)}) copy-start(bf16[4,4,120,512]{3,2,1,0:T(8,128)(2,1)} %get-tuple-element.8) | copy-start | bytes 5898244
  162.6 1.6 copy-start.24
  163.3 1.7 copy-start.23
  164.2 1.7 copy-start.22
  165.0 1.7 copy-start.21
  165.8 1.7 copy-start.20
  166.7 1.7 copy-start.19
  167.5 1.7 copy-start.18
  168.4 1.7 copy-start.17
  169.2 1.7 copy-start.16
  170.1 1.7 copy-start.15
  170.9 1.7 copy-start.14
  171.8 1.7 copy-start.13
  172.6 1.7 copy-start.12
  173.5 1.7 copy-start.11
  174.3 1.7 copy-start.10
  175.2 1.7 copy-start.9
  176.0 1.7 copy-start.7
  176.9 1.8 copy-start.6
  177.7 1.7 copy-start.5
  178.7 1.7 copy-start.4
  179.4 1.7 copy-start.3
  180.4 1.8 copy-start.2
  181.1 1.8 copy-start.1
  182.1 1.8 copy-start.8
Sparse Core Ops, SparseCore 0:
  21.8 86.8 all-gather.1
  158.4 126.6 reduce-scatter.1
where the time goes:
time: 292 us
  waiting for transfers between devices  113 us (39%)
  blocking collectives  71 us (24%)
  local copies, waits for them, and re-layouts  45.4 us (16%)
  matrix products  34.5 us (12%)
  between operations  14.3 us (5%)
  starting transfers between devices  10.8 us (4%)
    reduce_scatter x1, waiting for transfers between devices, local(): lax.psum_scatter(block, 'height', scatter_dimension=4, tiled=True)  97.9 us
    all_gather x1, blocking collectives, local(): kernel_all = lax.all_gather(kernel, 'height', axis=4, tiled=True)  71 us
    slice x2, local copies, waits for them, and re-layouts, tap_terms(): padded[2 - frame_tap:2 - frame_tap + frames, 2 - row_tap:2 - row_tap + ro...  25.3 us
    dot_general x27, matrix products, tap_terms(): lax.dot_general(shifted, kernel_part[:, frame_tap, row_tap, col_tap, :],...  21.1 us
    all_gather x1, waiting for transfers between devices, local(): lax.all_gather(rimmed, 'chan', axis=3, tiled=True)  14.1 us
    dot_general x27, matrix products, tap_terms(): lax.dot_general(x_rows, shifted, (((0,), (0,)), ((), ())), preferred_elem...  13.3 us
    ppermute x1, starting transfers between devices, padded_2(): after = lax.ppermute(initial, axis, down)  8.77 us
    unnamed x57, local copies, waits for them, and re-layouts  7.72 us
  transfers between devices with their start and end apart: 4, of which 3 were waited for; matrix products, arithmetic and copies ran while one was open for 8% of the time, Pallas kernels for 0%

commit v1 on v0

v1 whole, which is shorter than its diff:
```python
import jax
import jax.numpy as jnp
from jax import lax
from jax.experimental import pallas as pl
from jax.experimental.pallas import tpu as pltpu
from jax.sharding import Mesh, PartitionSpec as P

QB = 128
TAPS = 27
LANES = 128
COLS = 896
VMEM = 40 * 1024 * 1024
HEIGHT = ("a", "q", "c")
CHAN = ("b", "z")
f32 = jnp.float32
bf16 = jnp.bfloat16
f16 = jnp.float16
NT = (((1,), (1,)), ((), ()))


def call(body, out, scratch, flops, name, n_smem, n_in):
    smem = [pl.BlockSpec(memory_space=pltpu.SMEM)] * n_smem
    vmem = [pl.BlockSpec(memory_space=pltpu.VMEM)] * n_in
    outs = jax.tree.map(lambda _: pl.BlockSpec(memory_space=pltpu.VMEM), out)
    return pl.pallas_call(
        body,
        out_shape=out,
        in_specs=smem + vmem,
        out_specs=outs,
        scratch_shapes=scratch,
        compiler_params=pltpu.CompilerParams(vmem_limit_bytes=VMEM),
        cost_estimate=pl.CostEstimate(flops=flops, bytes_accessed=8000000, transcendentals=0),
        name=name,
    )


def frame_of(g_ref, t):
    blocks, _, rows, width, lanes = g_ref.shape
    return jnp.concatenate([g_ref[:, t, h].reshape(blocks * width, lanes) for h in range(rows)], axis=1)


def kernel_grad_body(where_ref, own_ref, other_ref, g_ref, keep_ref, send_ref, cols_ref, shifted_ref, acc_ref):
    half, core = where_ref[0], where_ref[1]
    frames, tall = own_ref.shape[:2]
    rows = tall - 2
    blocks = g_ref.shape[0]
    for ref, at in ((own_ref, half), (other_ref, 1 - half)):
        for s in range(frames):
            for r in range(tall):
                x = ref[s, r].astype(f32)
                cols_ref[0, s, r, at] = pltpu.roll(x, 1, 1).astype(bf16)
                cols_ref[1, s, r, at] = ref[s, r]
                cols_ref[2, s, r, at] = pltpu.roll(x, LANES - 1, 1).astype(bf16)
    shifted_ref[...] = jnp.zeros_like(shifted_ref)
    for t in range(frames):
        for tap in range(TAPS):
            a, b, c = tap // 9, tap // 3 % 3, tap % 3
            s = t - 2 + a
            if s < 0:
                continue
            for k in range(2):
                for h in range(rows):
                    shifted_ref[k * COLS + tap * 32:k * COLS + tap * 32 + 32, h * LANES:(h + 1) * LANES] = cols_ref[c, s, h + b, k]
        term = lax.dot_general(frame_of(g_ref, t), shifted_ref[...], NT, preferred_element_type=f32)
        term = term.reshape(blocks, 2, 16, 2 * COLS)
        if t == 0:
            acc_ref[...] = term
        else:
            acc_ref[...] += term
    for k in range(2):
        for q in range(blocks):
            keep_ref[k, q] = acc_ref[q, core, :, k * COLS:(k + 1) * COLS]
            send_ref[k, q] = acc_ref[q, 1 - core, :, k * COLS:(k + 1) * COLS]


def narrow_body(keep_ref, recv_ref, out_ref):
    total = keep_ref[...] + recv_ref[...]
    top = jnp.maximum(jnp.max(jnp.abs(total), keepdims=True), 2.0 ** -110)
    power = 14.0 - jnp.floor(jnp.log2(top))
    scaled = total * jnp.exp2(power)
    lane = lax.broadcasted_iota(jnp.int32, total.shape, len(total.shape) - 1)
    out = jnp.where(lane < TAPS * 32, scaled, power)
    out_ref[...] = out.reshape(out_ref.shape)


def widened(parts):
    parts = parts.astype(f32)
    return jnp.sum(parts * jnp.exp2(-parts[:, :, TAPS * 32:TAPS * 32 + 1]), axis=0)


def input_grad_body(where_ref, own_ref, other_ref, g_ref, keep_ref, send_ref, wide_ref, mats_ref, acc_ref):
    half, core = where_ref[0], where_ref[1]
    blocks, frames, rows = g_ref.shape[:3]
    for k in range(2):
        for q in range(blocks):
            wide_ref[k, q, core] = own_ref[k * blocks + q]
            wide_ref[k, q, 1 - core] = other_ref[k * blocks + q]
    for k in range(2):
        flat = wide_ref[k].reshape(blocks * 32, COLS).T
        for ab in range(9):
            mats_ref[ab, k * 96:k * 96 + 96] = flat[ab * 96:ab * 96 + 96]
    for s in range(frames):
        acc_ref[...] = jnp.zeros_like(acc_ref)
        for b in range(3):
            term = None
            for a in range(3):
                t = s + 2 - a
                if t >= frames:
                    continue
                one = jnp.dot(mats_ref[a * 3 + b], frame_of(g_ref, t), preferred_element_type=f32)
                term = one if term is None else term + one
            acc_ref[:, b * LANES:(b + rows) * LANES] += term
        for r in range(rows + 2):
            at = slice(r * LANES, (r + 1) * LANES)
            done = []
            for k in range(2):
                left = acc_ref[k * 96:k * 96 + 32, at]
                mid = acc_ref[k * 96 + 32:k * 96 + 64, at]
                right = acc_ref[k * 96 + 64:k * 96 + 96, at]
                done.append(mid + pltpu.roll(left, LANES - 1, 1) + pltpu.roll(right, 1, 1))
            first = half == 0
            keep_ref[s, r] = jnp.where(first, done[0], done[1])
            send_ref[s, r] = jnp.where(first, done[1], done[0])


def swap(axis, array):
    return lax.ppermute(array, axis, [(0, 1), (1, 0)])


def cross(array):
    return lax.ppermute(array, ("a", "b"), [(0, 0), (1, 2), (2, 1), (3, 3)])


def to_next(array):
    size = lax.axis_size(HEIGHT)
    return lax.ppermute(array, HEIGHT, [(i, i + 1) for i in range(size - 1)])


def to_prev(array):
    size = lax.axis_size(HEIGHT)
    return lax.ppermute(array, HEIGHT, [(i + 1, i) for i in range(size - 1)])


def lanes_padded(array):
    return jnp.pad(array, [(0, 0)] * (array.ndim - 1) + [(0, LANES - array.shape[-1])])


def local(saved, exponents, out_grad, kernel):
    frames, rows, width, ch = saved.shape
    zs = lax.axis_size("z")
    heights = lax.axis_size(("a", "q"))
    where = jnp.stack([lax.axis_index("b"), lax.axis_index("c")]).astype(jnp.int32)

    g_own = lanes_padded(out_grad.transpose(0, 1, 3, 2))
    g_all = lax.all_to_all(jnp.broadcast_to(g_own[None], (zs,) + g_own.shape), "z", 0, 0)

    first = lax.axis_index(CHAN) * ch // QB
    power = lax.dynamic_slice_in_dim(exponents.transpose(0, 1, 3, 2), first, 1, 2)
    x = saved.transpose(0, 1, 3, 2).astype(f32) * jnp.exp2(power.astype(f32))
    x = lanes_padded(x.astype(bf16))
    before, after = to_next(x[:, rows - 1:]), to_prev(x[:, :1])
    x_own = jnp.concatenate([before, x, after], axis=1)
    x_other = swap("b", x_own)

    flat = kernel.reshape(ch, TAPS, 16).transpose(2, 1, 0).reshape(16, TAPS * ch)
    flat = cross(jnp.pad(flat, ((0, 0), (0, COLS - TAPS * ch))))
    k_own = lax.all_to_all(jnp.broadcast_to(flat[None], (heights, 16, COLS)), ("a", "q"), 0, 0)
    k_other = swap("c", k_own)

    part = jax.ShapeDtypeStruct((2, zs, 16, COLS), f32)
    keep, send = call(
        kernel_grad_body,
        [part, part],
        [
            pltpu.VMEM((3, frames, rows + 2, 2, ch, LANES), bf16),
            pltpu.VMEM((2 * COLS, rows * LANES), bf16),
            pltpu.VMEM((zs, 2, 16, 2 * COLS), f32),
        ],
        2 * 2 * COLS * zs * 32 * frames * rows * LANES,
        "kernel_grad",
        1,
        3,
    )(where, x_own, x_other, g_all)
    parts = call(narrow_body, jax.ShapeDtypeStruct((heights, 16, COLS), f32), [], 1000000, "narrow", 0, 2)(keep, swap("c", send))
    parts = lax.all_to_all(parts.astype(f16), ("a", "q"), 0, 0)
    total = cross(widened(parts))[:, :TAPS * ch].reshape(16, TAPS, ch)
    kernel_grad = total.transpose(2, 1, 0).reshape(ch, 3, 3, 3, 16)

    grown = jax.ShapeDtypeStruct((frames, rows + 2, ch, LANES), f32)
    keep, send = call(
        input_grad_body,
        [grown, grown],
        [
            pltpu.VMEM((2, zs, 2, 16, COLS), bf16),
            pltpu.VMEM((9, 192, zs * 32), bf16),
            pltpu.VMEM((192, (rows + 2) * LANES), f32),
        ],
        2 * TAPS * 64 * zs * 32 * frames * rows * LANES,
        "input_grad",
        1,
        3,
    )(where, k_own, k_other, g_all)
    grown = keep + swap("b", send)
    above, below = to_next(grown[:, rows + 1]), to_prev(grown[:, 0])
    grad = grown[:, 1:rows + 1].at[:, 0].add(above).at[:, rows - 1].add(below)
    grad = grad[..., :width].astype(bf16).transpose(0, 1, 3, 2)
    return grad, kernel_grad


def solution(mesh):
    zs = mesh.shape["chan"] // 2
    fine = Mesh(mesh.devices.reshape(2, zs, 2, 2, zs), ("a", "q", "c", "b", "z"))
    in_specs = (
        P(None, HEIGHT, None, CHAN),
        P(None, HEIGHT, None, None),
        P(None, HEIGHT, None, CHAN),
        P(CHAN, None, None, None, HEIGHT),
    )
    out_specs = (P(None, HEIGHT, None, CHAN), P(CHAN, None, None, None, HEIGHT))
    return jax.shard_map(local, mesh=fine, in_specs=in_specs, out_specs=out_specs, check_vma=False)
```

time: 292 us -> 130 us (0.45)
  the two profiles are of different devices: /device:TPU:1 before, /device:TPU:31 now
where the time goes in v1:
time: 130 us; the launch traced here: 129 us
  starting transfers between devices  65.2 us (50%)
  waiting for transfers between devices  47.9 us (37%)
  Pallas kernels  7.99 us (6%)
  local copies, waits for them, and re-layouts  4.9 us (4%)
  other arithmetic  2.24 us (2%)
    all_to_all x1, waiting for transfers between devices, local(): lax.all_to_all(jnp.broadcast_to(g_own[None], (zs,) + g_own.shape), 'z', 0...  21.3 us
    ppermute x2, starting transfers between devices, to_next(): return lax.ppermute(array, HEIGHT, [(i, i + 1) for i in range(size - 1)])  17.8 us
    ppermute x2, waiting for transfers between devices, to_prev(): return lax.ppermute(array, HEIGHT, [(i + 1, i) for i in range(size - 1)])  13 us
    ppermute x4, starting transfers between devices, swap(): return lax.ppermute(array, axis, [(0, 1), (1, 0)])  10.4 us
    all_to_all x1, starting transfers between devices, local(): lax.all_to_all(jnp.broadcast_to(g_own[None], (zs,) + g_own.shape), 'z', 0...  10.2 us
    all_to_all x1, starting transfers between devices, local(): lax.all_to_all(jnp.broadcast_to(flat[None], (heights, 16, COLS)), ('a', '...  8.5 us
    ppermute x2, waiting for transfers between devices, cross(): return lax.ppermute(array, ('a', 'b'), [(0, 0), (1, 2), (2, 1), (3, 3)])  7.47 us
    all_to_all x1, starting transfers between devices, local(): parts = lax.all_to_all(parts.astype(f16), ('a', 'q'), 0, 0)  6.9 us
  transfers between devices with their start and end apart: 13, of which 8 were waited for; matrix products, arithmetic and copies ran while one was open for 2% of the time, Pallas kernels for 6%

profile of v1, /device:TPU:31, one launch (start us, length us, event | category | flops | bytes accessed | tf_op | source)
XLA Modules:
  0.0 129.2 jit_solution(17177539259685390565)
XLA Ops:
  0.6 0.9 pad.16
  1.6 1.2 broadcast_in_dim.5
  2.8 0.0 copy-start.3
  2.8 10.2 %all-to-all-start.1 = ((bf16[8,4,4,32,128]{4,3,2,1,0:T(8,128)(2,1)}), bf16[8,4,4,32,128]{4,3,2,1,0:T(8,128)(2,1)S(1)}, u32[]{:S(2)}, u32[]{:S(2)}) async-start(bf16[8,4,4,32,128]{4,3,2,1,0:T(8,128)(2,1)} %broadcast_in_dim.5), calls=%async_computation.1 | async-start | bytes 2097152 | tf_op jit(solution)/shard_map/all_to_all | solution.py:155
  13.0 0.0 copy-done.3
  13.0 0.2 reshape.102
  13.2 4.6 %collective-permute-start = (bf16[16,896]{1,0:T(8,128)(2,1)S(1)}, bf16[16,896]{1,0:T(8,128)(2,1)S(1)}, u32[]{:S(2)}, u32[]{:S(2)}) collective-permute-start(bf16[16,896]{1,0:T(8,128)(2,1)S(1)} %pad.15), channel_id=1, source_target_pairs={{0,0},{8,256},{256,8},{264,264},{1,1},{9,257},{257,9},{265,265},{2... | collective-permute-start | bytes 86024 | tf_op jit(solution)/shard_map/ppermute | solution.py:131
  17.9 0.8 multiply_exponential_fusion
  18.6 2.2 %collective-permute-done = bf16[16,896]{1,0:T(8,128)(2,1)S(1)} collective-permute-done((bf16[16,896]{1,0:T(8,128)(2,1)S(1)}, bf16[16,896]{1,0:T(8,128)(2,1)S(1)}, u32[]{:S(2)}, u32[]{:S(2)}) %collective-permute-start) | collective-permute-done | bytes 28704 | tf_op jit(solution)/shard_map/ppermute | solution.py:131
  20.8 21.3 %all-to-all-done.1.g_ref = bf16[8,4,4,32,128]{4,3,2,1,0:T(8,128)(2,1)S(1)} async-done(((bf16[8,4,4,32,128]{4,3,2,1,0:T(8,128)(2,1)}), bf16[8,4,4,32,128]{4,3,2,1,0:T(8,128)(2,1)S(1)}, u32[]{:S(2)}, u32[]{:S(2)}) %all-to-all-start.1) | async-done | bytes 1048608 | tf_op jit(solution)/shard_map/all_to_all | solution.py:155
  42.1 0.8 broadcast_in_dim.4
  43.0 8.5 %all-to-all-start = ((bf16[16,16,896]{2,1,0:T(8,128)(2,1)}), bf16[16,16,896]{2,1,0:T(8,128)(2,1)S(1)}, u32[]{:S(2)}, u32[]{:S(2)}) async-start(bf16[16,16,896]{2,1,0:T(8,128)(2,1)} %broadcast_in_dim.4), calls=%async_computation | async-start | bytes 917504 | tf_op jit(solution)/shard_map/all_to_all | solution.py:167
  51.5 0.0 copy-done.2
  51.5 3.0 %collective-permute-start.6 = (bf16[4,1,32,128]{3,2,1,0:T(8,128)(2,1)S(1)}, bf16[4,1,32,128]{3,2,1,0:T(8,128)(2,1)S(1)}, u32[]{:S(2)}, u32[]{:S(2)}) collective-permute-start(bf16[4,1,32,128]{3,2,1,0:T(8,128)(2,1)S(1)} %get-tuple-element.43), channel_id=1, source_target_pairs={{16,0},{32,16},{48,32},{64,48},{80,64},{96,80},{112,96},{128,112},... | collective-permute-start | bytes 98312 | tf_op jit(solution)/shard_map/ppermute | solution.py:141
  54.5 6.8 %collective-permute-start.5 = (bf16[4,1,32,128]{3,2,1,0:T(8,128)(2,1)S(1)}, bf16[4,1,32,128]{3,2,1,0:T(8,128)(2,1)S(1)}, u32[]{:S(2)}, u32[]{:S(2)}) collective-permute-start(bf16[4,1,32,128]{3,2,1,0:T(8,128)(2,1)S(1)} %get-tuple-element.42), channel_id=1, source_target_pairs={{0,16},{16,32},{32,48},{48,64},{64,80},{80,96},{96,112},{112,128},... | collective-permute-start | bytes 98312 | tf_op jit(solution)/shard_map/ppermute | solution.py:136
  61.4 5.2 %collective-permute-done.6 = bf16[4,1,32,128]{3,2,1,0:T(8,128)(2,1)S(1)} collective-permute-done((bf16[4,1,32,128]{3,2,1,0:T(8,128)(2,1)S(1)}, bf16[4,1,32,128]{3,2,1,0:T(8,128)(2,1)S(1)}, u32[]{:S(2)}, u32[]{:S(2)}) %collective-permute-start.6) | collective-permute-done | bytes 32800 | tf_op jit(solution)/shard_map/ppermute | solution.py:141
  66.5 0.0 collective-permute-done.5
  66.6 3.0 %collective-permute-start.7 = (bf16[4,6,32,128]{3,2,1,0:T(8,128)(2,1)S(1)}, bf16[4,6,32,128]{3,2,1,0:T(8,128)(2,1)S(1)}, u32[]{:S(2)}, u32[]{:S(2)}) collective-permute-start(bf16[4,6,32,128]{3,2,1,0:T(8,128)(2,1)S(1)} %pad_maximum_fusion.own_ref), channel_id=1, source_target_pairs={{0,8},{8,0},{1,9},{9,1},{2,10},{10,2},{3,11},{11,3},{4,12},{12,4},... | collective-permute-start | bytes 589832 | tf_op jit(solution)/shard_map/ppermute | solution.py:127
  69.6 0.1 pad_add_fusion.where_ref
  69.7 3.3 %collective-permute-done.7.other_ref = bf16[4,6,32,128]{3,2,1,0:T(8,128)(2,1)S(1)} collective-permute-done((bf16[4,6,32,128]{3,2,1,0:T(8,128)(2,1)S(1)}, bf16[4,6,32,128]{3,2,1,0:T(8,128)(2,1)S(1)}, u32[]{:S(2)}, u32[]{:S(2)}) %collective-permute-start.7) | collective-permute-done | bytes 196640 | tf_op jit(solution)/shard_map/ppermute | solution.py:127
  73.0 4.7 %kernel_grad.1 = (f32[2,8,16,896]{3,2,1,0:T(8,128)S(1)}, f32[2,8,16,896]{3,2,1,0:T(8,128)}) custom-call(s32[2]{0:T(128)S(1)} %pad_add_fusion.where_ref, bf16[4,6,32,128]{3,2,1,0:T(8,128)(2,1)S(1)} %pad_maximum_fusion.own_ref, bf16[4,6,32,128]{3,2,1,0:T(8,128)(2,1)S(1)} %collective-permute-done.7.other_ref, bf16[8,4,4,32,128]{4,3,2,1,0:T(8,128)(2,1)S(1)} %all-to-all-done.1.g_ref), custom_call_target="tpu_custom_call" | custom-call | flops 1879048192 | bytes 8000000 | tf_op jit(solution)/shard_map/kernel_grad/pallas_call | solution.py:171
  77.7 1.9 %collective-permute-start.8 = (f32[2,8,16,896]{3,2,1,0:T(8,128)}, f32[2,8,16,896]{3,2,1,0:T(8,128)S(1)}, u32[]{:S(2)}, u32[]{:S(2)}) collective-permute-start(f32[2,8,16,896]{3,2,1,0:T(8,128)} %get-tuple-element.33), channel_id=1, source_target_pairs={{0,16},{16,0},{1,17},{17,1},{2,18},{18,2},{3,19},{19,3},{4,20},{20... | collective-permute-start | bytes 2752520 | tf_op jit(solution)/shard_map/ppermute | solution.py:127
  79.6 0.0 all-to-all-done.own_ref
  79.6 2.4 %collective-permute-start.1 = (bf16[16,16,896]{2,1,0:T(8,128)(2,1)S(1)}, bf16[16,16,896]{2,1,0:T(8,128)(2,1)S(1)}, u32[]{:S(2)}, u32[]{:S(2)}) collective-permute-start(bf16[16,16,896]{2,1,0:T(8,128)(2,1)S(1)} %all-to-all-done.own_ref), channel_id=1, source_target_pairs={{0,16},{16,0},{1,17},{17,1},{2,18},{18,2},{3,19},{19,3},{4,20},{20... | collective-permute-start | bytes 1376264 | tf_op jit(solution)/shard_map/ppermute | solution.py:127
  82.0 1.4 %collective-permute-done.1.other_ref = bf16[16,16,896]{2,1,0:T(8,128)(2,1)S(1)} collective-permute-done((bf16[16,16,896]{2,1,0:T(8,128)(2,1)S(1)}, bf16[16,16,896]{2,1,0:T(8,128)(2,1)S(1)}, u32[]{:S(2)}, u32[]{:S(2)}) %collective-permute-start.1) | collective-permute-done | bytes 458784 | tf_op jit(solution)/shard_map/ppermute | solution.py:127
  83.4 3.1 %input_grad.1 = (f32[4,6,32,128]{3,2,1,0:T(8,128)S(1)}, f32[4,6,32,128]{3,2,1,0:T(8,128)}) custom-call(s32[2]{0:T(128)S(1)} %pad_add_fusion.where_ref, bf16[16,16,896]{2,1,0:T(8,128)(2,1)S(1)} %all-to-all-done.own_ref, bf16[16,16,896]{2,1,0:T(8,128)(2,1)S(1)} %collective-permute-done.1.other_ref, bf16[8,4,4,32,128]{4,3,2,1,0:T(8,128)(2,1)S(1)} %all-to-all-done.1.g_ref), custom_call_target="tpu_custom_call" | custom-call | flops 1811939328 | bytes 8000000 | tf_op jit(solution)/shard_map/input_grad/pallas_call | solution.py:190
  86.5 3.0 %collective-permute-start.2 = (f32[4,6,32,128]{3,2,1,0:T(8,128)}, f32[4,6,32,128]{3,2,1,0:T(8,128)S(1)}, u32[]{:S(2)}, u32[]{:S(2)}) collective-permute-start(f32[4,6,32,128]{3,2,1,0:T(8,128)} %get-tuple-element.31), channel_id=1, source_target_pairs={{0,8},{8,0},{1,9},{9,1},{2,10},{10,2},{3,11},{11,3},{4,12},{12,4},... | collective-permute-start | bytes 1179656 | tf_op jit(solution)/shard_map/ppermute | solution.py:127
  89.5 0.0 collective-permute-done.8.recv_ref
  89.5 0.3 narrow.1
  89.8 0.0 copy-done
  89.8 0.8 convert_element_type.34
  90.6 6.9 %all-to-all-start.2 = ((f16[16,16,896]{2,1,0:T(8,128)(2,1)}), f16[16,16,896]{2,1,0:T(8,128)(2,1)S(1)}, u32[]{:S(2)}, u32[]{:S(2)}) async-start(f16[16,16,896]{2,1,0:T(8,128)(2,1)} %convert_element_type.34), calls=%async_computation.2 | async-start | bytes 917504 | tf_op jit(solution)/shard_map/all_to_all | solution.py:185
  97.5 1.4 %collective-permute-done.2 = f32[4,6,32,128]{3,2,1,0:T(8,128)S(1)} collective-permute-done((f32[4,6,32,128]{3,2,1,0:T(8,128)}, f32[4,6,32,128]{3,2,1,0:T(8,128)S(1)}, u32[]{:S(2)}, u32[]{:S(2)}) %collective-permute-start.2) | collective-permute-done | bytes 393248 | tf_op jit(solution)/shard_map/ppermute | solution.py:127
  98.9 0.0 copy-done.1
  98.9 0.1 add.30
  99.0 11.0 %collective-permute-start.3 = (f32[4,32,128]{2,1,0:T(8,128)S(1)}, f32[4,32,128]{2,1,0:T(8,128)S(1)}, u32[]{:S(2)}, u32[]{:S(2)}) collective-permute-start(f32[4,32,128]{2,1,0:T(8,128)S(1)} %get-tuple-element.41), channel_id=1, source_target_pairs={{0,16},{16,32},{32,48},{48,64},{64,80},{80,96},{96,112},{112,128},... | collective-permute-start | bytes 196616 | tf_op jit(solution)/shard_map/ppermute | solution.py:136
  110.0 1.9 %collective-permute-start.4 = (f32[4,32,128]{2,1,0:T(8,128)S(1)}, f32[4,32,128]{2,1,0:T(8,128)S(1)}, u32[]{:S(2)}, u32[]{:S(2)}) collective-permute-start(f32[4,32,128]{2,1,0:T(8,128)S(1)} %get-tuple-element.40), channel_id=1, source_target_pairs={{16,0},{32,16},{48,32},{64,48},{80,64},{96,80},{112,96},{128,112},... | collective-permute-start | bytes 196616 | tf_op jit(solution)/shard_map/ppermute | solution.py:141
  112.0 0.0 collective-permute-done.3
  112.0 7.8 %collective-permute-done.4 = f32[4,32,128]{2,1,0:T(8,128)S(1)} collective-permute-done((f32[4,32,128]{2,1,0:T(8,128)S(1)}, f32[4,32,128]{2,1,0:T(8,128)S(1)}, u32[]{:S(2)}, u32[]{:S(2)}) %collective-permute-start.4) | collective-permute-done | bytes 65568 | tf_op jit(solution)/shard_map/ppermute | solution.py:141
  119.8 0.0 all-to-all-done.2
  119.9 0.1 convert_element_type.35
  119.9 0.2 fusion.4
  120.1 0.2 multiply_reduce_fusion
  120.3 1.9 %collective-permute-start.9 = (f32[16,896]{1,0:T(8,128)S(1)}, f32[16,896]{1,0:T(8,128)S(1)}, u32[]{:S(2)}, u32[]{:S(2)}) collective-permute-start(f32[16,896]{1,0:T(8,128)S(1)} %multiply_reduce_fusion), channel_id=1, source_target_pairs={{0,0},{8,256},{256,8},{264,264},{1,1},{9,257},{257,9},{265,265},{2... | collective-permute-start | bytes 172040 | tf_op jit(solution)/shard_map/ppermute | solution.py:131
  122.2 0.7 copy.22
  122.9 5.3 %collective-permute-done.9 = f32[16,896]{1,0:T(8,128)S(1)} collective-permute-done((f32[16,896]{1,0:T(8,128)S(1)}, f32[16,896]{1,0:T(8,128)S(1)}, u32[]{:S(2)}, u32[]{:S(2)}) %collective-permute-start.9) | collective-permute-done | bytes 57376 | tf_op jit(solution)/shard_map/ppermute | solution.py:131
  128.2 0.1 reshape.105
  128.3 0.8 copy.21
  (15 shorter events, 0.2 us)
Async XLA Ops:
  2.8 10.2 %copy-start.3 = (bf16[32,3,3,3,16]{0,4,3,2,1:T(8,128)(2,1)S(1)}, bf16[32,3,3,3,16]{0,4,3,2,1:T(8,128)(2,1)}, u32[]{:S(2)}) copy-start(bf16[32,3,3,3,16]{0,4,3,2,1:T(8,128)(2,1)} %param.11) | copy-start | bytes 82948
  2.8 39.4 %all-to-all-start.1 = ((bf16[8,4,4,32,128]{4,3,2,1,0:T(8,128)(2,1)}), bf16[8,4,4,32,128]{4,3,2,1,0:T(8,128)(2,1)S(1)}, u32[]{:S(2)}, u32[]{:S(2)}) async-start(bf16[8,4,4,32,128]{4,3,2,1,0:T(8,128)(2,1)} %broadcast_in_dim.5), calls=%async_computation.1 | async-start | bytes 2097152 | tf_op jit(solution)/shard_map/all_to_all | solution.py:155
  13.2 7.6 %collective-permute-start = (bf16[16,896]{1,0:T(8,128)(2,1)S(1)}, bf16[16,896]{1,0:T(8,128)(2,1)S(1)}, u32[]{:S(2)}, u32[]{:S(2)}) collective-permute-start(bf16[16,896]{1,0:T(8,128)(2,1)S(1)} %pad.15), channel_id=1, source_target_pairs={{0,0},{8,256},{256,8},{264,264},{1,1},{9,257},{257,9},{265,265},{2... | collective-permute-start | bytes 86024 | tf_op jit(solution)/shard_map/ppermute | solution.py:131
  43.0 8.5 %copy-start.2 = (s32[4,4,120,32]{2,3,1,0:T(8,128)S(1)}, s32[4,4,120,32]{2,3,1,0:T(8,128)}, u32[]{:S(2)}) copy-start(s32[4,4,120,32]{2,3,1,0:T(8,128)} %param.8) | copy-start | bytes 737284
  43.0 36.6 %all-to-all-start = ((bf16[16,16,896]{2,1,0:T(8,128)(2,1)}), bf16[16,16,896]{2,1,0:T(8,128)(2,1)S(1)}, u32[]{:S(2)}, u32[]{:S(2)}) async-start(bf16[16,16,896]{2,1,0:T(8,128)(2,1)} %broadcast_in_dim.4), calls=%async_computation | async-start | bytes 917504 | tf_op jit(solution)/shard_map/all_to_all | solution.py:167
  51.5 15.0 %collective-permute-start.6 = (bf16[4,1,32,128]{3,2,1,0:T(8,128)(2,1)S(1)}, bf16[4,1,32,128]{3,2,1,0:T(8,128)(2,1)S(1)}, u32[]{:S(2)}, u32[]{:S(2)}) collective-permute-start(bf16[4,1,32,128]{3,2,1,0:T(8,128)(2,1)S(1)} %get-tuple-element.43), channel_id=1, source_target_pairs={{16,0},{32,16},{48,32},{64,48},{80,64},{96,80},{112,96},{128,112},... | collective-permute-start | bytes 98312 | tf_op jit(solution)/shard_map/ppermute | solution.py:141
  54.5 12.0 %collective-permute-start.5 = (bf16[4,1,32,128]{3,2,1,0:T(8,128)(2,1)S(1)}, bf16[4,1,32,128]{3,2,1,0:T(8,128)(2,1)S(1)}, u32[]{:S(2)}, u32[]{:S(2)}) collective-permute-start(bf16[4,1,32,128]{3,2,1,0:T(8,128)(2,1)S(1)} %get-tuple-element.42), channel_id=1, source_target_pairs={{0,16},{16,32},{32,48},{48,64},{64,80},{80,96},{96,112},{112,128},... | collective-permute-start | bytes 98312 | tf_op jit(solution)/shard_map/ppermute | solution.py:136
  66.6 6.4 %collective-permute-start.7 = (bf16[4,6,32,128]{3,2,1,0:T(8,128)(2,1)S(1)}, bf16[4,6,32,128]{3,2,1,0:T(8,128)(2,1)S(1)}, u32[]{:S(2)}, u32[]{:S(2)}) collective-permute-start(bf16[4,6,32,128]{3,2,1,0:T(8,128)(2,1)S(1)} %pad_maximum_fusion.own_ref), channel_id=1, source_target_pairs={{0,8},{8,0},{1,9},{9,1},{2,10},{10,2},{3,11},{11,3},{4,12},{12,4},... | collective-permute-start | bytes 589832 | tf_op jit(solution)/shard_map/ppermute | solution.py:127
  77.7 11.8 %collective-permute-start.8 = (f32[2,8,16,896]{3,2,1,0:T(8,128)}, f32[2,8,16,896]{3,2,1,0:T(8,128)S(1)}, u32[]{:S(2)}, u32[]{:S(2)}) collective-permute-start(f32[2,8,16,896]{3,2,1,0:T(8,128)} %get-tuple-element.33), channel_id=1, source_target_pairs={{0,16},{16,0},{1,17},{17,1},{2,18},{18,2},{3,19},{19,3},{4,20},{20... | collective-permute-start | bytes 2752520 | tf_op jit(solution)/shard_map/ppermute | solution.py:127
  79.6 3.8 %collective-permute-start.1 = (bf16[16,16,896]{2,1,0:T(8,128)(2,1)S(1)}, bf16[16,16,896]{2,1,0:T(8,128)(2,1)S(1)}, u32[]{:S(2)}, u32[]{:S(2)}) collective-permute-start(bf16[16,16,896]{2,1,0:T(8,128)(2,1)S(1)} %all-to-all-done.own_ref), channel_id=1, source_target_pairs={{0,16},{16,0},{1,17},{17,1},{2,18},{18,2},{3,19},{19,3},{4,20},{20... | collective-permute-start | bytes 1376264 | tf_op jit(solution)/shard_map/ppermute | solution.py:127
  86.5 3.3 %copy-start = (f32[4,6,32,128]{3,2,1,0:T(8,128)}, f32[4,6,32,128]{3,2,1,0:T(8,128)S(1)}, u32[]{:S(2)}) copy-start(f32[4,6,32,128]{3,2,1,0:T(8,128)S(1)} %get-tuple-element.30) | copy-start | bytes 1179652
  86.5 12.4 %collective-permute-start.2 = (f32[4,6,32,128]{3,2,1,0:T(8,128)}, f32[4,6,32,128]{3,2,1,0:T(8,128)S(1)}, u32[]{:S(2)}, u32[]{:S(2)}) collective-permute-start(f32[4,6,32,128]{3,2,1,0:T(8,128)} %get-tuple-element.31), channel_id=1, source_target_pairs={{0,8},{8,0},{1,9},{9,1},{2,10},{10,2},{3,11},{11,3},{4,12},{12,4},... | collective-permute-start | bytes 1179656 | tf_op jit(solution)/shard_map/ppermute | solution.py:127
  90.6 8.3 %copy-start.1 = (f32[4,6,32,128]{3,2,1,0:T(8,128)S(1)}, f32[4,6,32,128]{3,2,1,0:T(8,128)}, u32[]{:S(2)}) copy-start(f32[4,6,32,128]{3,2,1,0:T(8,128)} %copy-done) | copy-start | bytes 1179652
  90.6 29.2 %all-to-all-start.2 = ((f16[16,16,896]{2,1,0:T(8,128)(2,1)}), f16[16,16,896]{2,1,0:T(8,128)(2,1)S(1)}, u32[]{:S(2)}, u32[]{:S(2)}) async-start(f16[16,16,896]{2,1,0:T(8,128)(2,1)} %convert_element_type.34), calls=%async_computation.2 | async-start | bytes 917504 | tf_op jit(solution)/shard_map/all_to_all | solution.py:185
  99.0 13.0 %collective-permute-start.3 = (f32[4,32,128]{2,1,0:T(8,128)S(1)}, f32[4,32,128]{2,1,0:T(8,128)S(1)}, u32[]{:S(2)}, u32[]{:S(2)}) collective-permute-start(f32[4,32,128]{2,1,0:T(8,128)S(1)} %get-tuple-element.41), channel_id=1, source_target_pairs={{0,16},{16,32},{32,48},{48,64},{64,80},{80,96},{96,112},{112,128},... | collective-permute-start | bytes 196616 | tf_op jit(solution)/shard_map/ppermute | solution.py:136
  110.0 9.8 %collective-permute-start.4 = (f32[4,32,128]{2,1,0:T(8,128)S(1)}, f32[4,32,128]{2,1,0:T(8,128)S(1)}, u32[]{:S(2)}, u32[]{:S(2)}) collective-permute-start(f32[4,32,128]{2,1,0:T(8,128)S(1)} %get-tuple-element.40), channel_id=1, source_target_pairs={{16,0},{32,16},{48,32},{64,48},{80,64},{96,80},{112,96},{128,112},... | collective-permute-start | bytes 196616 | tf_op jit(solution)/shard_map/ppermute | solution.py:141
  120.3 7.9 %collective-permute-start.9 = (f32[16,896]{1,0:T(8,128)S(1)}, f32[16,896]{1,0:T(8,128)S(1)}, u32[]{:S(2)}, u32[]{:S(2)}) collective-permute-start(f32[16,896]{1,0:T(8,128)S(1)} %multiply_reduce_fusion), channel_id=1, source_target_pairs={{0,0},{8,256},{256,8},{264,264},{1,1},{9,257},{257,9},{265,265},{2... | collective-permute-start | bytes 172040 | tf_op jit(solution)/shard_map/ppermute | solution.py:131

commit v2 on v1

--- a/solution.py
+++ b/solution.py
@@ -89,12 +89,11 @@
 
 
 def input_grad_body(where_ref, own_ref, other_ref, g_ref, keep_ref, send_ref, wide_ref, mats_ref, acc_ref):
-    half, core = where_ref[0], where_ref[1]
+    half, core, high, place = where_ref[0], where_ref[1], where_ref[2], where_ref[3]
     blocks, frames, rows = g_ref.shape[:3]
-    for k in range(2):
-        for q in range(blocks):
-            wide_ref[k, q, core] = own_ref[k * blocks + q]
-            wide_ref[k, q, 1 - core] = other_ref[k * blocks + q]
+    for j, (k, q) in enumerate(gather_order(blocks)):
+        wide_ref[high ^ k, place ^ q, core] = own_ref[j]
+        wide_ref[high ^ k, place ^ q, 1 - core] = other_ref[j]
     for k in range(2):
         flat = wide_ref[k].reshape(blocks * 32, COLS).T
         for ab in range(9):
@@ -131,6 +130,30 @@
     return lax.ppermute(array, ("a", "b"), [(0, 0), (1, 2), (2, 1), (3, 3)])
 
 
+def cross_other(array):
+    return lax.ppermute(array, ("a", "b"), [(0, 2), (1, 0), (2, 3), (3, 1)])
+
+
+def strides(size):
+    return [1 << bit for bit in reversed(range(size.bit_length() - 1))]
+
+
+def gather_order(size):
+    order = [(0, 0), (1, 0)]
+    for stride in strides(size):
+        order = order + [(k, q | stride) for k, q in order]
+    return order
+
+
+def gathered(array):
+    size = lax.axis_size("q")
+    array = jnp.stack([cross(array), cross_other(array)])
+    for stride in strides(size):
+        other = lax.ppermute(array, "q", [(i, i ^ stride) for i in range(size)])
+        array = jnp.concatenate([array, other])
+    return array
+
+
 def to_next(array):
     size = lax.axis_size(HEIGHT)
     return lax.ppermute(array, HEIGHT, [(i, i + 1) for i in range(size - 1)])
@@ -149,7 +172,7 @@
     frames, rows, width, ch = saved.shape
     zs = lax.axis_size("z")
     heights = lax.axis_size(("a", "q"))
-    where = jnp.stack([lax.axis_index("b"), lax.axis_index("c")]).astype(jnp.int32)
+    where = jnp.stack([lax.axis_index(axis) for axis in "bcaq"]).astype(jnp.int32)
 
     g_own = lanes_padded(out_grad.transpose(0, 1, 3, 2))
     g_all = lax.all_to_all(jnp.broadcast_to(g_own[None], (zs,) + g_own.shape), "z", 0, 0)
@@ -163,8 +186,7 @@
     x_other = swap("b", x_own)
 
     flat = kernel.reshape(ch, TAPS, 16).transpose(2, 1, 0).reshape(16, TAPS * ch)
-    flat = cross(jnp.pad(flat, ((0, 0), (0, COLS - TAPS * ch))))
-    k_own = lax.all_to_all(jnp.broadcast_to(flat[None], (heights, 16, COLS)), ("a", "q"), 0, 0)
+    k_own = gathered(jnp.pad(flat, ((0, 0), (0, COLS - TAPS * ch))))
     k_other = swap("c", k_own)
 
     part = jax.ShapeDtypeStruct((2, zs, 16, COLS), f32)

time: 130 us -> 101 us (0.78)
  the two profiles are of different devices: /device:TPU:31 before, /device:TPU:79 now
where the time goes in v2:
time: 101 us
  starting transfers between devices  66.6 us (66%)
  waiting for transfers between devices  20.4 us (20%)
  Pallas kernels  6.28 us (6%)
  local copies, waits for them, and re-layouts  4.15 us (4%)
  other arithmetic  2.3 us (2%)
  between operations  1.03 us (1%)
    ppermute x2, starting transfers between devices, to_next(): return lax.ppermute(array, HEIGHT, [(i, i + 1) for i in range(size - 1)])  14.3 us
    ppermute x4, starting transfers between devices, swap(): return lax.ppermute(array, axis, [(0, 1), (1, 0)])  12.4 us
    all_to_all x1, starting transfers between devices, local(): lax.all_to_all(jnp.broadcast_to(g_own[None], (zs,) + g_own.shape), 'z', 0...  9.54 us
    ppermute x2, starting transfers between devices, cross(): return lax.ppermute(array, ('a', 'b'), [(0, 0), (1, 2), (2, 1), (3, 3)])  8.36 us
    ppermute x3, starting transfers between devices, gathered(): other = lax.ppermute(array, 'q', [(i, i ^ stride) for i in range(size)])  8.25 us
    ppermute x2, waiting for transfers between devices, to_prev(): return lax.ppermute(array, HEIGHT, [(i + 1, i) for i in range(size - 1)])  7.34 us
    all_to_all x1, starting transfers between devices, local(): parts = lax.all_to_all(parts.astype(f16), ('a', 'q'), 0, 0)  6.48 us
    ppermute x2, starting transfers between devices, to_prev(): return lax.ppermute(array, HEIGHT, [(i + 1, i) for i in range(size - 1)])  5.34 us
  transfers between devices with their start and end apart: 16, of which 7 were waited for; matrix products, arithmetic and copies ran while one was open for 3% of the time, Pallas kernels for 6%

profile of v2, /device:TPU:79, one launch (start us, length us, event | category | flops | bytes accessed | tf_op | source)
XLA Modules:
  0.0 100.8 jit_solution(7415312746973818287)
XLA Ops:
  0.6 0.9 pad.16
  1.6 1.2 %broadcast_in_dim.2 = bf16[8,4,4,32,128]{4,3,2,1,0:T(8,128)(2,1)} broadcast(bf16[4,4,32,128]{3,2,1,0:T(8,128)(2,1)S(1)} %pad.16), dimensions={1,2,3,4} | broadcast | bytes 1179648 | tf_op jit(solution)/shard_map/broadcast_in_dim | solution.py:178
  2.8 9.5 %all-to-all-start = ((bf16[8,4,4,32,128]{4,3,2,1,0:T(8,128)(2,1)}), bf16[8,4,4,32,128]{4,3,2,1,0:T(8,128)(2,1)S(1)}, u32[]{:S(2)}, u32[]{:S(2)}) async-start(bf16[8,4,4,32,128]{4,3,2,1,0:T(8,128)(2,1)} %broadcast_in_dim.2), calls=%async_computation | async-start | bytes 2097152 | tf_op jit(solution)/shard_map/all_to_all | solution.py:178
  12.4 0.2 reshape.101
  12.5 6.4 %collective-permute-start = (bf16[16,896]{1,0:T(8,128)(2,1)S(1)}, bf16[16,896]{1,0:T(8,128)(2,1)S(1)}, u32[]{:S(2)}, u32[]{:S(2)}) collective-permute-start(bf16[16,896]{1,0:T(8,128)(2,1)S(1)} %pad.15), channel_id=1, source_target_pairs={{0,0},{8,256},{256,8},{264,264},{1,1},{9,257},{257,9},{265,265},{2... | collective-permute-start | bytes 86024 | tf_op jit(solution)/shard_map/ppermute | solution.py:130
  19.0 1.9 %collective-permute-start.1 = (bf16[16,896]{1,0:T(8,128)(2,1)S(1)}, bf16[16,896]{1,0:T(8,128)(2,1)S(1)}, u32[]{:S(2)}, u32[]{:S(2)}) collective-permute-start(bf16[16,896]{1,0:T(8,128)(2,1)S(1)} %pad.15), channel_id=1, source_target_pairs={{0,256},{8,0},{256,264},{264,8},{1,257},{9,1},{257,265},{265,9},{2... | collective-permute-start | bytes 86024 | tf_op jit(solution)/shard_map/ppermute | solution.py:134
  20.9 0.8 multiply_exponential_fusion
  21.8 3.4 %collective-permute-start.10 = (bf16[4,1,32,128]{3,2,1,0:T(8,128)(2,1)S(1)}, bf16[4,1,32,128]{3,2,1,0:T(8,128)(2,1)S(1)}, u32[]{:S(2)}, u32[]{:S(2)}) collective-permute-start(bf16[4,1,32,128]{3,2,1,0:T(8,128)(2,1)S(1)} %get-tuple-element.43), channel_id=1, source_target_pairs={{16,0},{32,16},{48,32},{64,48},{80,64},{96,80},{112,96},{128,112},... | collective-permute-start | bytes 98312 | tf_op jit(solution)/shard_map/ppermute | solution.py:164
  25.2 5.1 %collective-permute-start.9 = (bf16[4,1,32,128]{3,2,1,0:T(8,128)(2,1)S(1)}, bf16[4,1,32,128]{3,2,1,0:T(8,128)(2,1)S(1)}, u32[]{:S(2)}, u32[]{:S(2)}) collective-permute-start(bf16[4,1,32,128]{3,2,1,0:T(8,128)(2,1)S(1)} %get-tuple-element.42), channel_id=1, source_target_pairs={{0,16},{16,32},{32,48},{48,64},{64,80},{80,96},{96,112},{112,128},... | collective-permute-start | bytes 98312 | tf_op jit(solution)/shard_map/ppermute | solution.py:159
  30.4 0.1 pad_add_fusion.where_ref
  30.5 0.0 collective-permute-done
  30.5 0.0 collective-permute-done.1
  30.6 4.4 %collective-permute-start.2 = (bf16[2,16,896]{2,1,0:T(8,128)(2,1)S(1)}, bf16[2,16,896]{2,1,0:T(8,128)(2,1)S(1)}, u32[]{:S(2)}, u32[]{:S(2)}) collective-permute-start(bf16[2,16,896]{2,1,0:T(8,128)(2,1)S(1)} %pad_maximum_fusion.3), channel_id=1, source_target_pairs={{0,128},{32,160},{64,192},{96,224},{128,0},{160,32},{192,64},{224,... | collective-permute-start | bytes 172040 | tf_op jit(solution)/shard_map/ppermute | solution.py:152
  35.0 2.4 %collective-permute-done.2 = bf16[2,16,896]{2,1,0:T(8,128)(2,1)S(1)} collective-permute-done((bf16[2,16,896]{2,1,0:T(8,128)(2,1)S(1)}, bf16[2,16,896]{2,1,0:T(8,128)(2,1)S(1)}, u32[]{:S(2)}, u32[]{:S(2)}) %collective-permute-start.2) | collective-permute-done | bytes 57376 | tf_op jit(solution)/shard_map/ppermute | solution.py:152
  37.4 1.9 %collective-permute-start.3 = (bf16[4,16,896]{2,1,0:T(8,128)(2,1)S(1)}, bf16[4,16,896]{2,1,0:T(8,128)(2,1)S(1)}, u32[]{:S(2)}, u32[]{:S(2)}) collective-permute-start(bf16[4,16,896]{2,1,0:T(8,128)(2,1)S(1)} %pad_maximum_fusion.2), channel_id=1, source_target_pairs={{0,64},{32,96},{64,0},{96,32},{128,192},{160,224},{192,128},{224,1... | collective-permute-start | bytes 344072 | tf_op jit(solution)/shard_map/ppermute | solution.py:152
  39.3 0.0 collective-permute-done.10
  39.3 0.0 collective-permute-done.9
  39.4 3.7 %collective-permute-start.11 = (bf16[4,6,32,128]{3,2,1,0:T(8,128)(2,1)S(1)}, bf16[4,6,32,128]{3,2,1,0:T(8,128)(2,1)S(1)}, u32[]{:S(2)}, u32[]{:S(2)}) collective-permute-start(bf16[4,6,32,128]{3,2,1,0:T(8,128)(2,1)S(1)} %pad_maximum_fusion.1.own_ref), channel_id=1, source_target_pairs={{0,8},{8,0},{1,9},{9,1},{2,10},{10,2},{3,11},{11,3},{4,12},{12,4},... | collective-permute-start | bytes 589832 | tf_op jit(solution)/shard_map/ppermute | solution.py:126
  43.1 2.0 %collective-permute-done.3 = bf16[4,16,896]{2,1,0:T(8,128)(2,1)S(1)} collective-permute-done((bf16[4,16,896]{2,1,0:T(8,128)(2,1)S(1)}, bf16[4,16,896]{2,1,0:T(8,128)(2,1)S(1)}, u32[]{:S(2)}, u32[]{:S(2)}) %collective-permute-start.3) | collective-permute-done | bytes 114720 | tf_op jit(solution)/shard_map/ppermute | solution.py:152
  45.1 1.9 %collective-permute-start.4 = (bf16[8,16,896]{2,1,0:T(8,128)(2,1)S(1)}, bf16[8,16,896]{2,1,0:T(8,128)(2,1)S(1)}, u32[]{:S(2)}, u32[]{:S(2)}) collective-permute-start(bf16[8,16,896]{2,1,0:T(8,128)(2,1)S(1)} %pad_maximum_fusion), channel_id=1, source_target_pairs={{0,32},{32,0},{64,96},{96,64},{128,160},{160,128},{192,224},{224,1... | collective-permute-start | bytes 688136 | tf_op jit(solution)/shard_map/ppermute | solution.py:152
  47.1 0.7 collective-permute-done.11.other_ref
  47.8 0.0 all-to-all-done.g_ref
  47.8 3.7 %kernel_grad.1 = (f32[2,8,16,896]{3,2,1,0:T(8,128)S(1)}, f32[2,8,16,896]{3,2,1,0:T(8,128)S(1)}) custom-call(s32[4]{0:T(128)S(1)} %pad_add_fusion.where_ref, bf16[4,6,32,128]{3,2,1,0:T(8,128)(2,1)S(1)} %pad_maximum_fusion.1.own_ref, bf16[4,6,32,128]{3,2,1,0:T(8,128)(2,1)S(1)} %collective-permute-done.11.other_ref, ...), custom_call_target="tpu_custom_call" | custom-call | flops 1879048192 | bytes 8000000 | tf_op jit(solution)/shard_map/kernel_grad/pallas_call | solution.py:193
  51.5 3.1 %collective-permute-start.12 = (f32[2,8,16,896]{3,2,1,0:T(8,128)S(1)}, f32[2,8,16,896]{3,2,1,0:T(8,128)S(1)}, u32[]{:S(2)}, u32[]{:S(2)}) collective-permute-start(f32[2,8,16,896]{3,2,1,0:T(8,128)S(1)} %get-tuple-element.33), channel_id=1, source_target_pairs={{0,16},{16,0},{1,17},{17,1},{2,18},{18,2},{3,19},{19,3},{4,20},{20... | collective-permute-start | bytes 2752520 | tf_op jit(solution)/shard_map/ppermute | solution.py:126
  54.6 0.0 collective-permute-done.4
  54.6 2.3 %collective-permute-start.5 = (bf16[16,16,896]{2,1,0:T(8,128)(2,1)S(1)}, bf16[16,16,896]{2,1,0:T(8,128)(2,1)S(1)}, u32[]{:S(2)}, u32[]{:S(2)}) collective-permute-start(bf16[16,16,896]{2,1,0:T(8,128)(2,1)S(1)} %constant_dynamic-update-slice_fusion.own_ref), channel_id=1, source_target_pairs={{0,16},{16,0},{1,17},{17,1},{2,18},{18,2},{3,19},{19,3},{4,20},{20... | collective-permute-start | bytes 1376264 | tf_op jit(solution)/shard_map/ppermute | solution.py:126
  57.0 1.4 %collective-permute-done.5.other_ref = bf16[16,16,896]{2,1,0:T(8,128)(2,1)S(1)} collective-permute-done((bf16[16,16,896]{2,1,0:T(8,128)(2,1)S(1)}, bf16[16,16,896]{2,1,0:T(8,128)(2,1)S(1)}, u32[]{:S(2)}, u32[]{:S(2)}) %collective-permute-start.5) | collective-permute-done | bytes 458784 | tf_op jit(solution)/shard_map/ppermute | solution.py:126
  58.4 2.3 %input_grad.1 = (f32[4,6,32,128]{3,2,1,0:T(8,128)S(1)}, f32[4,6,32,128]{3,2,1,0:T(8,128)S(1)}) custom-call(s32[4]{0:T(128)S(1)} %pad_add_fusion.where_ref, bf16[16,16,896]{2,1,0:T(8,128)(2,1)S(1)} %constant_dynamic-update-slice_fusion.own_ref, bf16[16,16,896]{2,1,0:T(8,128)(2,1)S(1)} %collective-permute-done.5.other_ref, ...), custom_call_target="tpu_custom_call" | custom-call | flops 1811939328 | bytes 8000000 | tf_op jit(solution)/shard_map/input_grad/pallas_call | solution.py:212
  60.7 3.3 %collective-permute-start.6 = (f32[4,6,32,128]{3,2,1,0:T(8,128)S(1)}, f32[4,6,32,128]{3,2,1,0:T(8,128)S(1)}, u32[]{:S(2)}, u32[]{:S(2)}) collective-permute-start(f32[4,6,32,128]{3,2,1,0:T(8,128)S(1)} %get-tuple-element.31), channel_id=1, source_target_pairs={{0,8},{8,0},{1,9},{9,1},{2,10},{10,2},{3,11},{11,3},{4,12},{12,4},... | collective-permute-start | bytes 1179656 | tf_op jit(solution)/shard_map/ppermute | solution.py:126
  64.0 0.0 collective-permute-done.12.recv_ref
  64.0 0.3 narrow.1
  64.3 0.8 convert_element_type.34
  65.1 6.5 %all-to-all-start.1 = ((f16[16,16,896]{2,1,0:T(8,128)(2,1)}), f16[16,16,896]{2,1,0:T(8,128)(2,1)S(1)}, u32[]{:S(2)}, u32[]{:S(2)}) async-start(f16[16,16,896]{2,1,0:T(8,128)(2,1)} %convert_element_type.34), calls=%async_computation.1 | async-start | bytes 917504 | tf_op jit(solution)/shard_map/all_to_all | solution.py:207
  71.6 1.3 %collective-permute-done.6 = f32[4,6,32,128]{3,2,1,0:T(8,128)S(1)} collective-permute-done((f32[4,6,32,128]{3,2,1,0:T(8,128)S(1)}, f32[4,6,32,128]{3,2,1,0:T(8,128)S(1)}, u32[]{:S(2)}, u32[]{:S(2)}) %collective-permute-start.6) | collective-permute-done | bytes 393248 | tf_op jit(solution)/shard_map/ppermute | solution.py:126
  72.9 0.1 add.30
  73.0 9.1 %collective-permute-start.7 = (f32[4,32,128]{2,1,0:T(8,128)S(1)}, f32[4,32,128]{2,1,0:T(8,128)S(1)}, u32[]{:S(2)}, u32[]{:S(2)}) collective-permute-start(f32[4,32,128]{2,1,0:T(8,128)S(1)} %get-tuple-element.41), channel_id=1, source_target_pairs={{0,16},{16,32},{32,48},{48,64},{64,80},{80,96},{96,112},{112,128},... | collective-permute-start | bytes 196616 | tf_op jit(solution)/shard_map/ppermute | solution.py:159
  82.2 1.9 %collective-permute-start.8 = (f32[4,32,128]{2,1,0:T(8,128)S(1)}, f32[4,32,128]{2,1,0:T(8,128)S(1)}, u32[]{:S(2)}, u32[]{:S(2)}) collective-permute-start(f32[4,32,128]{2,1,0:T(8,128)S(1)} %get-tuple-element.40), channel_id=1, source_target_pairs={{16,0},{32,16},{48,32},{64,48},{80,64},{96,80},{112,96},{128,112},... | collective-permute-start | bytes 196616 | tf_op jit(solution)/shard_map/ppermute | solution.py:164
  84.1 0.0 collective-permute-done.7
  84.1 7.3 %collective-permute-done.8 = f32[4,32,128]{2,1,0:T(8,128)S(1)} collective-permute-done((f32[4,32,128]{2,1,0:T(8,128)S(1)}, f32[4,32,128]{2,1,0:T(8,128)S(1)}, u32[]{:S(2)}, u32[]{:S(2)}) %collective-permute-start.8) | collective-permute-done | bytes 65568 | tf_op jit(solution)/shard_map/ppermute | solution.py:164
  91.5 0.0 all-to-all-done.1
  91.5 0.1 convert_element_type.35
  91.6 0.2 fusion.4
  91.8 0.2 multiply_reduce_fusion
  91.9 1.9 %collective-permute-start.13 = (f32[16,896]{1,0:T(8,128)S(1)}, f32[16,896]{1,0:T(8,128)S(1)}, u32[]{:S(2)}, u32[]{:S(2)}) collective-permute-start(f32[16,896]{1,0:T(8,128)S(1)} %multiply_reduce_fusion), channel_id=1, source_target_pairs={{0,0},{8,256},{256,8},{264,264},{1,1},{9,257},{257,9},{265,265},{2... | collective-permute-start | bytes 172040 | tf_op jit(solution)/shard_map/ppermute | solution.py:130
  93.9 0.7 copy.22
  94.5 5.3 %collective-permute-done.13 = f32[16,896]{1,0:T(8,128)S(1)} collective-permute-done((f32[16,896]{1,0:T(8,128)S(1)}, f32[16,896]{1,0:T(8,128)S(1)}, u32[]{:S(2)}, u32[]{:S(2)}) %collective-permute-start.13) | collective-permute-done | bytes 57376 | tf_op jit(solution)/shard_map/ppermute | solution.py:130
  99.8 0.1 reshape.104
  100.0 0.8 copy.21
  (24 shorter events, 0.4 us)
Async XLA Ops:
  2.8 9.5 %copy-start.1 = (bf16[32,3,3,3,16]{0,4,3,2,1:T(8,128)(2,1)S(1)}, bf16[32,3,3,3,16]{0,4,3,2,1:T(8,128)(2,1)}, u32[]{:S(2)}) copy-start(bf16[32,3,3,3,16]{0,4,3,2,1:T(8,128)(2,1)} %param.11) | copy-start | bytes 82948
  2.8 45.0 %all-to-all-start = ((bf16[8,4,4,32,128]{4,3,2,1,0:T(8,128)(2,1)}), bf16[8,4,4,32,128]{4,3,2,1,0:T(8,128)(2,1)S(1)}, u32[]{:S(2)}, u32[]{:S(2)}) async-start(bf16[8,4,4,32,128]{4,3,2,1,0:T(8,128)(2,1)} %broadcast_in_dim.2), calls=%async_computation | async-start | bytes 2097152 | tf_op jit(solution)/shard_map/all_to_all | solution.py:178
  12.3 9.4 %copy-start = (s32[4,4,120,32]{2,3,1,0:T(8,128)S(1)}, s32[4,4,120,32]{2,3,1,0:T(8,128)}, u32[]{:S(2)}) copy-start(s32[4,4,120,32]{2,3,1,0:T(8,128)} %param.8) | copy-start | bytes 737284
  12.5 18.0 %collective-permute-start = (bf16[16,896]{1,0:T(8,128)(2,1)S(1)}, bf16[16,896]{1,0:T(8,128)(2,1)S(1)}, u32[]{:S(2)}, u32[]{:S(2)}) collective-permute-start(bf16[16,896]{1,0:T(8,128)(2,1)S(1)} %pad.15), channel_id=1, source_target_pairs={{0,0},{8,256},{256,8},{264,264},{1,1},{9,257},{257,9},{265,265},{2... | collective-permute-start | bytes 86024 | tf_op jit(solution)/shard_map/ppermute | solution.py:130
  19.0 11.5 %collective-permute-start.1 = (bf16[16,896]{1,0:T(8,128)(2,1)S(1)}, bf16[16,896]{1,0:T(8,128)(2,1)S(1)}, u32[]{:S(2)}, u32[]{:S(2)}) collective-permute-start(bf16[16,896]{1,0:T(8,128)(2,1)S(1)} %pad.15), channel_id=1, source_target_pairs={{0,256},{8,0},{256,264},{264,8},{1,257},{9,1},{257,265},{265,9},{2... | collective-permute-start | bytes 86024 | tf_op jit(solution)/shard_map/ppermute | solution.py:134
  21.8 17.5 %collective-permute-start.10 = (bf16[4,1,32,128]{3,2,1,0:T(8,128)(2,1)S(1)}, bf16[4,1,32,128]{3,2,1,0:T(8,128)(2,1)S(1)}, u32[]{:S(2)}, u32[]{:S(2)}) collective-permute-start(bf16[4,1,32,128]{3,2,1,0:T(8,128)(2,1)S(1)} %get-tuple-element.43), channel_id=1, source_target_pairs={{16,0},{32,16},{48,32},{64,48},{80,64},{96,80},{112,96},{128,112},... | collective-permute-start | bytes 98312 | tf_op jit(solution)/shard_map/ppermute | solution.py:164
  25.2 14.1 %collective-permute-start.9 = (bf16[4,1,32,128]{3,2,1,0:T(8,128)(2,1)S(1)}, bf16[4,1,32,128]{3,2,1,0:T(8,128)(2,1)S(1)}, u32[]{:S(2)}, u32[]{:S(2)}) collective-permute-start(bf16[4,1,32,128]{3,2,1,0:T(8,128)(2,1)S(1)} %get-tuple-element.42), channel_id=1, source_target_pairs={{0,16},{16,32},{32,48},{48,64},{64,80},{80,96},{96,112},{112,128},... | collective-permute-start | bytes 98312 | tf_op jit(solution)/shard_map/ppermute | solution.py:159
  30.6 6.8 %collective-permute-start.2 = (bf16[2,16,896]{2,1,0:T(8,128)(2,1)S(1)}, bf16[2,16,896]{2,1,0:T(8,128)(2,1)S(1)}, u32[]{:S(2)}, u32[]{:S(2)}) collective-permute-start(bf16[2,16,896]{2,1,0:T(8,128)(2,1)S(1)} %pad_maximum_fusion.3), channel_id=1, source_target_pairs={{0,128},{32,160},{64,192},{96,224},{128,0},{160,32},{192,64},{224,... | collective-permute-start | bytes 172040 | tf_op jit(solution)/shard_map/ppermute | solution.py:152
  37.4 7.7 %collective-permute-start.3 = (bf16[4,16,896]{2,1,0:T(8,128)(2,1)S(1)}, bf16[4,16,896]{2,1,0:T(8,128)(2,1)S(1)}, u32[]{:S(2)}, u32[]{:S(2)}) collective-permute-start(bf16[4,16,896]{2,1,0:T(8,128)(2,1)S(1)} %pad_maximum_fusion.2), channel_id=1, source_target_pairs={{0,64},{32,96},{64,0},{96,32},{128,192},{160,224},{192,128},{224,1... | collective-permute-start | bytes 344072 | tf_op jit(solution)/shard_map/ppermute | solution.py:152
  39.4 8.4 %collective-permute-start.11 = (bf16[4,6,32,128]{3,2,1,0:T(8,128)(2,1)S(1)}, bf16[4,6,32,128]{3,2,1,0:T(8,128)(2,1)S(1)}, u32[]{:S(2)}, u32[]{:S(2)}) collective-permute-start(bf16[4,6,32,128]{3,2,1,0:T(8,128)(2,1)S(1)} %pad_maximum_fusion.1.own_ref), channel_id=1, source_target_pairs={{0,8},{8,0},{1,9},{9,1},{2,10},{10,2},{3,11},{11,3},{4,12},{12,4},... | collective-permute-start | bytes 589832 | tf_op jit(solution)/shard_map/ppermute | solution.py:126
  45.1 9.5 %collective-permute-start.4 = (bf16[8,16,896]{2,1,0:T(8,128)(2,1)S(1)}, bf16[8,16,896]{2,1,0:T(8,128)(2,1)S(1)}, u32[]{:S(2)}, u32[]{:S(2)}) collective-permute-start(bf16[8,16,896]{2,1,0:T(8,128)(2,1)S(1)} %pad_maximum_fusion), channel_id=1, source_target_pairs={{0,32},{32,0},{64,96},{96,64},{128,160},{160,128},{192,224},{224,1... | collective-permute-start | bytes 688136 | tf_op jit(solution)/shard_map/ppermute | solution.py:152
  51.5 12.5 %collective-permute-start.12 = (f32[2,8,16,896]{3,2,1,0:T(8,128)S(1)}, f32[2,8,16,896]{3,2,1,0:T(8,128)S(1)}, u32[]{:S(2)}, u32[]{:S(2)}) collective-permute-start(f32[2,8,16,896]{3,2,1,0:T(8,128)S(1)} %get-tuple-element.33), channel_id=1, source_target_pairs={{0,16},{16,0},{1,17},{17,1},{2,18},{18,2},{3,19},{19,3},{4,20},{20... | collective-permute-start | bytes 2752520 | tf_op jit(solution)/shard_map/ppermute | solution.py:126
  54.6 3.8 %collective-permute-start.5 = (bf16[16,16,896]{2,1,0:T(8,128)(2,1)S(1)}, bf16[16,16,896]{2,1,0:T(8,128)(2,1)S(1)}, u32[]{:S(2)}, u32[]{:S(2)}) collective-permute-start(bf16[16,16,896]{2,1,0:T(8,128)(2,1)S(1)} %constant_dynamic-update-slice_fusion.own_ref), channel_id=1, source_target_pairs={{0,16},{16,0},{1,17},{17,1},{2,18},{18,2},{3,19},{19,3},{4,20},{20... | collective-permute-start | bytes 1376264 | tf_op jit(solution)/shard_map/ppermute | solution.py:126
  60.7 12.2 %collective-permute-start.6 = (f32[4,6,32,128]{3,2,1,0:T(8,128)S(1)}, f32[4,6,32,128]{3,2,1,0:T(8,128)S(1)}, u32[]{:S(2)}, u32[]{:S(2)}) collective-permute-start(f32[4,6,32,128]{3,2,1,0:T(8,128)S(1)} %get-tuple-element.31), channel_id=1, source_target_pairs={{0,8},{8,0},{1,9},{9,1},{2,10},{10,2},{3,11},{11,3},{4,12},{12,4},... | collective-permute-start | bytes 1179656 | tf_op jit(solution)/shard_map/ppermute | solution.py:126
  65.1 26.3 %all-to-all-start.1 = ((f16[16,16,896]{2,1,0:T(8,128)(2,1)}), f16[16,16,896]{2,1,0:T(8,128)(2,1)S(1)}, u32[]{:S(2)}, u32[]{:S(2)}) async-start(f16[16,16,896]{2,1,0:T(8,128)(2,1)} %convert_element_type.34), calls=%async_computation.1 | async-start | bytes 917504 | tf_op jit(solution)/shard_map/all_to_all | solution.py:207
  73.0 11.1 %collective-permute-start.7 = (f32[4,32,128]{2,1,0:T(8,128)S(1)}, f32[4,32,128]{2,1,0:T(8,128)S(1)}, u32[]{:S(2)}, u32[]{:S(2)}) collective-permute-start(f32[4,32,128]{2,1,0:T(8,128)S(1)} %get-tuple-element.41), channel_id=1, source_target_pairs={{0,16},{16,32},{32,48},{48,64},{64,80},{80,96},{96,112},{112,128},... | collective-permute-start | bytes 196616 | tf_op jit(solution)/shard_map/ppermute | solution.py:159
  82.2 9.3 %collective-permute-start.8 = (f32[4,32,128]{2,1,0:T(8,128)S(1)}, f32[4,32,128]{2,1,0:T(8,128)S(1)}, u32[]{:S(2)}, u32[]{:S(2)}) collective-permute-start(f32[4,32,128]{2,1,0:T(8,128)S(1)} %get-tuple-element.40), channel_id=1, source_target_pairs={{16,0},{32,16},{48,32},{64,48},{80,64},{96,80},{112,96},{128,112},... | collective-permute-start | bytes 196616 | tf_op jit(solution)/shard_map/ppermute | solution.py:164
  91.9 7.9 %collective-permute-start.13 = (f32[16,896]{1,0:T(8,128)S(1)}, f32[16,896]{1,0:T(8,128)S(1)}, u32[]{:S(2)}, u32[]{:S(2)}) collective-permute-start(f32[16,896]{1,0:T(8,128)S(1)} %multiply_reduce_fusion), channel_id=1, source_target_pairs={{0,0},{8,256},{256,8},{264,264},{1,1},{9,257},{257,9},{265,265},{2... | collective-permute-start | bytes 172040 | tf_op jit(solution)/shard_map/ppermute | solution.py:130

commit v3 on v2

--- a/solution.py
+++ b/solution.py
@@ -51,22 +51,26 @@
                 cols_ref[0, s, r, at] = pltpu.roll(x, 1, 1).astype(bf16)
                 cols_ref[1, s, r, at] = ref[s, r]
                 cols_ref[2, s, r, at] = pltpu.roll(x, LANES - 1, 1).astype(bf16)
-    shifted_ref[...] = jnp.zeros_like(shifted_ref)
-    for t in range(frames):
-        for tap in range(TAPS):
-            a, b, c = tap // 9, tap // 3 % 3, tap % 3
-            s = t - 2 + a
-            if s < 0:
-                continue
-            for k in range(2):
+    for t in reversed(range(frames)):
+        low = max(0, 2 - t) * 9
+        start = low * 32 // LANES * LANES
+        for k in range(2):
+            for tap in range(start // 32, TAPS + 1):
+                at = k * COLS + tap * 32
+                if tap < low or tap == TAPS:
+                    shifted_ref[at:at + 32] = jnp.zeros((32, rows * LANES), bf16)
+                    continue
+                a, b, c = tap // 9, tap // 3 % 3, tap % 3
                 for h in range(rows):
-                    shifted_ref[k * COLS + tap * 32:k * COLS + tap * 32 + 32, h * LANES:(h + 1) * LANES] = cols_ref[c, s, h + b, k]
-        term = lax.dot_general(frame_of(g_ref, t), shifted_ref[...], NT, preferred_element_type=f32)
-        term = term.reshape(blocks, 2, 16, 2 * COLS)
-        if t == 0:
-            acc_ref[...] = term
-        else:
-            acc_ref[...] += term
+                    shifted_ref[at:at + 32, h * LANES:(h + 1) * LANES] = cols_ref[c, t - 2 + a, h + b, k]
+        g = frame_of(g_ref, t)
+        for at, end in [(0, 2 * COLS)] if start == 0 else [(start, COLS), (COLS + start, 2 * COLS)]:
+            term = lax.dot_general(g, shifted_ref[at:end], NT, preferred_element_type=f32)
+            term = term.reshape(blocks, 2, 16, end - at)
+            if t == frames - 1:
+                acc_ref[...] = term
+            else:
+                acc_ref[:, :, :, at:end] += term
     for k in range(2):
         for q in range(blocks):
             keep_ref[k, q] = acc_ref[q, core, :, k * COLS:(k + 1) * COLS]

time: 101 us -> 101 us (level)
  the two profiles are of different devices: /device:TPU:79 before, /device:TPU:31 now
where the time goes in v3:
time: 101 us; the launch traced here: 99.8 us
  starting transfers between devices  63.7 us (63%)
  waiting for transfers between devices  22.7 us (22%)
  Pallas kernels  5.98 us (6%)
  local copies, waits for them, and re-layouts  4.15 us (4%)
  other arithmetic  2.3 us (2%)
  between operations  1.03 us (1%)
    ppermute x2, starting transfers between devices, to_next(): return lax.ppermute(array, HEIGHT, [(i, i + 1) for i in range(size - 1)])  14.6 us
    ppermute x4, starting transfers between devices, swap(): return lax.ppermute(array, axis, [(0, 1), (1, 0)])  11.7 us
    all_to_all x1, starting transfers between devices, local(): lax.all_to_all(jnp.broadcast_to(g_own[None], (zs,) + g_own.shape), 'z', 0...  10.2 us
    all_to_all x1, starting transfers between devices, local(): parts = lax.all_to_all(parts.astype(f16), ('a', 'q'), 0, 0)  7.73 us
    ppermute x2, starting transfers between devices, cross(): return lax.ppermute(array, ('a', 'b'), [(0, 0), (1, 2), (2, 1), (3, 3)])  6.56 us
    ppermute x2, waiting for transfers between devices, to_prev(): return lax.ppermute(array, HEIGHT, [(i + 1, i) for i in range(size - 1)])  6.43 us
    ppermute x3, starting transfers between devices, gathered(): other = lax.ppermute(array, 'q', [(i, i ^ stride) for i in range(size)])  5.9 us
    ppermute x3, waiting for transfers between devices, gathered(): other = lax.ppermute(array, 'q', [(i, i ^ stride) for i in range(size)])  5.63 us
  transfers between devices with their start and end apart: 16, of which 8 were waited for; matrix products, arithmetic and copies ran while one was open for 3% of the time, Pallas kernels for 6%

profile of v3, /device:TPU:31, one launch (start us, length us, event | category | flops | bytes accessed | tf_op | source)
XLA Modules:
  0.0 99.8 jit_solution(7090993591693143711)
XLA Ops:
  0.6 0.9 pad.16
  1.6 1.2 %broadcast_in_dim.2 = bf16[8,4,4,32,128]{4,3,2,1,0:T(8,128)(2,1)} broadcast(bf16[4,4,32,128]{3,2,1,0:T(8,128)(2,1)S(1)} %pad.16), dimensions={1,2,3,4} | broadcast | bytes 1179648 | tf_op jit(solution)/shard_map/broadcast_in_dim | solution.py:182
  2.8 10.2 %all-to-all-start = ((bf16[8,4,4,32,128]{4,3,2,1,0:T(8,128)(2,1)}), bf16[8,4,4,32,128]{4,3,2,1,0:T(8,128)(2,1)S(1)}, u32[]{:S(2)}, u32[]{:S(2)}) async-start(bf16[8,4,4,32,128]{4,3,2,1,0:T(8,128)(2,1)} %broadcast_in_dim.2), calls=%async_computation | async-start | bytes 2097152 | tf_op jit(solution)/shard_map/all_to_all | solution.py:182
  13.0 0.0 copy-start
  13.0 0.2 reshape.101
  13.2 4.6 %collective-permute-start = (bf16[16,896]{1,0:T(8,128)(2,1)S(1)}, bf16[16,896]{1,0:T(8,128)(2,1)S(1)}, u32[]{:S(2)}, u32[]{:S(2)}) collective-permute-start(bf16[16,896]{1,0:T(8,128)(2,1)S(1)} %pad.15), channel_id=1, source_target_pairs={{0,0},{8,256},{256,8},{264,264},{1,1},{9,257},{257,9},{265,265},{2... | collective-permute-start | bytes 86024 | tf_op jit(solution)/shard_map/ppermute | solution.py:134
  17.8 1.9 %collective-permute-start.1 = (bf16[16,896]{1,0:T(8,128)(2,1)S(1)}, bf16[16,896]{1,0:T(8,128)(2,1)S(1)}, u32[]{:S(2)}, u32[]{:S(2)}) collective-permute-start(bf16[16,896]{1,0:T(8,128)(2,1)S(1)} %pad.15), channel_id=1, source_target_pairs={{0,256},{8,0},{256,264},{264,8},{1,257},{9,1},{257,265},{265,9},{2... | collective-permute-start | bytes 86024 | tf_op jit(solution)/shard_map/ppermute | solution.py:138
  19.8 0.8 multiply_exponential_fusion
  20.7 3.1 %collective-permute-start.10 = (bf16[4,1,32,128]{3,2,1,0:T(8,128)(2,1)S(1)}, bf16[4,1,32,128]{3,2,1,0:T(8,128)(2,1)S(1)}, u32[]{:S(2)}, u32[]{:S(2)}) collective-permute-start(bf16[4,1,32,128]{3,2,1,0:T(8,128)(2,1)S(1)} %get-tuple-element.43), channel_id=1, source_target_pairs={{16,0},{32,16},{48,32},{64,48},{80,64},{96,80},{112,96},{128,112},... | collective-permute-start | bytes 98312 | tf_op jit(solution)/shard_map/ppermute | solution.py:168
  23.8 7.1 %collective-permute-start.9 = (bf16[4,1,32,128]{3,2,1,0:T(8,128)(2,1)S(1)}, bf16[4,1,32,128]{3,2,1,0:T(8,128)(2,1)S(1)}, u32[]{:S(2)}, u32[]{:S(2)}) collective-permute-start(bf16[4,1,32,128]{3,2,1,0:T(8,128)(2,1)S(1)} %get-tuple-element.42), channel_id=1, source_target_pairs={{0,16},{16,32},{32,48},{48,64},{64,80},{80,96},{96,112},{112,128},... | collective-permute-start | bytes 98312 | tf_op jit(solution)/shard_map/ppermute | solution.py:163
  31.0 0.1 pad_add_fusion.where_ref
  31.1 0.0 collective-permute-done
  31.1 0.0 collective-permute-done.1
  31.1 2.1 %collective-permute-start.2 = (bf16[2,16,896]{2,1,0:T(8,128)(2,1)S(1)}, bf16[2,16,896]{2,1,0:T(8,128)(2,1)S(1)}, u32[]{:S(2)}, u32[]{:S(2)}) collective-permute-start(bf16[2,16,896]{2,1,0:T(8,128)(2,1)S(1)} %pad_maximum_fusion.3), channel_id=1, source_target_pairs={{0,128},{32,160},{64,192},{96,224},{128,0},{160,32},{192,64},{224,... | collective-permute-start | bytes 172040 | tf_op jit(solution)/shard_map/ppermute | solution.py:156
  33.2 4.0 %collective-permute-done.2 = bf16[2,16,896]{2,1,0:T(8,128)(2,1)S(1)} collective-permute-done((bf16[2,16,896]{2,1,0:T(8,128)(2,1)S(1)}, bf16[2,16,896]{2,1,0:T(8,128)(2,1)S(1)}, u32[]{:S(2)}, u32[]{:S(2)}) %collective-permute-start.2) | collective-permute-done | bytes 57376 | tf_op jit(solution)/shard_map/ppermute | solution.py:156
  37.2 1.9 %collective-permute-start.3 = (bf16[4,16,896]{2,1,0:T(8,128)(2,1)S(1)}, bf16[4,16,896]{2,1,0:T(8,128)(2,1)S(1)}, u32[]{:S(2)}, u32[]{:S(2)}) collective-permute-start(bf16[4,16,896]{2,1,0:T(8,128)(2,1)S(1)} %pad_maximum_fusion.2), channel_id=1, source_target_pairs={{0,64},{32,96},{64,0},{96,32},{128,192},{160,224},{192,128},{224,1... | collective-permute-start | bytes 344072 | tf_op jit(solution)/shard_map/ppermute | solution.py:156
  39.2 0.0 collective-permute-done.10
  39.2 0.0 collective-permute-done.9
  39.2 4.3 %collective-permute-start.11 = (bf16[4,6,32,128]{3,2,1,0:T(8,128)(2,1)S(1)}, bf16[4,6,32,128]{3,2,1,0:T(8,128)(2,1)S(1)}, u32[]{:S(2)}, u32[]{:S(2)}) collective-permute-start(bf16[4,6,32,128]{3,2,1,0:T(8,128)(2,1)S(1)} %pad_maximum_fusion.1.own_ref), channel_id=1, source_target_pairs={{0,8},{8,0},{1,9},{9,1},{2,10},{10,2},{3,11},{11,3},{4,12},{12,4},... | collective-permute-start | bytes 589832 | tf_op jit(solution)/shard_map/ppermute | solution.py:130
  43.6 1.6 %collective-permute-done.3 = bf16[4,16,896]{2,1,0:T(8,128)(2,1)S(1)} collective-permute-done((bf16[4,16,896]{2,1,0:T(8,128)(2,1)S(1)}, bf16[4,16,896]{2,1,0:T(8,128)(2,1)S(1)}, u32[]{:S(2)}, u32[]{:S(2)}) %collective-permute-start.3) | collective-permute-done | bytes 114720 | tf_op jit(solution)/shard_map/ppermute | solution.py:156
  45.2 1.9 %collective-permute-start.4 = (bf16[8,16,896]{2,1,0:T(8,128)(2,1)S(1)}, bf16[8,16,896]{2,1,0:T(8,128)(2,1)S(1)}, u32[]{:S(2)}, u32[]{:S(2)}) collective-permute-start(bf16[8,16,896]{2,1,0:T(8,128)(2,1)S(1)} %pad_maximum_fusion), channel_id=1, source_target_pairs={{0,32},{32,0},{64,96},{96,64},{128,160},{160,128},{192,224},{224,1... | collective-permute-start | bytes 688136 | tf_op jit(solution)/shard_map/ppermute | solution.py:156
  47.2 1.2 %collective-permute-done.11.other_ref = bf16[4,6,32,128]{3,2,1,0:T(8,128)(2,1)S(1)} collective-permute-done((bf16[4,6,32,128]{3,2,1,0:T(8,128)(2,1)S(1)}, bf16[4,6,32,128]{3,2,1,0:T(8,128)(2,1)S(1)}, u32[]{:S(2)}, u32[]{:S(2)}) %collective-permute-start.11) | collective-permute-done | bytes 196640 | tf_op jit(solution)/shard_map/ppermute | solution.py:130
  48.3 3.4 %kernel_grad.1 = (f32[2,8,16,896]{3,2,1,0:T(8,128)S(1)}, f32[2,8,16,896]{3,2,1,0:T(8,128)S(1)}) custom-call(s32[4]{0:T(128)S(1)} %pad_add_fusion.where_ref, bf16[4,6,32,128]{3,2,1,0:T(8,128)(2,1)S(1)} %pad_maximum_fusion.1.own_ref, bf16[4,6,32,128]{3,2,1,0:T(8,128)(2,1)S(1)} %collective-permute-done.11.other_ref, ...), custom_call_target="tpu_custom_call" | custom-call | flops 1879048192 | bytes 8000000 | tf_op jit(solution)/shard_map/kernel_grad/pallas_call | solution.py:197
  51.8 3.0 %collective-permute-start.12 = (f32[2,8,16,896]{3,2,1,0:T(8,128)S(1)}, f32[2,8,16,896]{3,2,1,0:T(8,128)S(1)}, u32[]{:S(2)}, u32[]{:S(2)}) collective-permute-start(f32[2,8,16,896]{3,2,1,0:T(8,128)S(1)} %get-tuple-element.33), channel_id=1, source_target_pairs={{0,16},{16,0},{1,17},{17,1},{2,18},{18,2},{3,19},{19,3},{4,20},{20... | collective-permute-start | bytes 2752520 | tf_op jit(solution)/shard_map/ppermute | solution.py:130
  54.7 0.0 collective-permute-done.4
  54.8 2.3 %collective-permute-start.5 = (bf16[16,16,896]{2,1,0:T(8,128)(2,1)S(1)}, bf16[16,16,896]{2,1,0:T(8,128)(2,1)S(1)}, u32[]{:S(2)}, u32[]{:S(2)}) collective-permute-start(bf16[16,16,896]{2,1,0:T(8,128)(2,1)S(1)} %constant_dynamic-update-slice_fusion.own_ref), channel_id=1, source_target_pairs={{0,16},{16,0},{1,17},{17,1},{2,18},{18,2},{3,19},{19,3},{4,20},{20... | collective-permute-start | bytes 1376264 | tf_op jit(solution)/shard_map/ppermute | solution.py:130
  57.1 1.4 %collective-permute-done.5.other_ref = bf16[16,16,896]{2,1,0:T(8,128)(2,1)S(1)} collective-permute-done((bf16[16,16,896]{2,1,0:T(8,128)(2,1)S(1)}, bf16[16,16,896]{2,1,0:T(8,128)(2,1)S(1)}, u32[]{:S(2)}, u32[]{:S(2)}) %collective-permute-start.5) | collective-permute-done | bytes 458784 | tf_op jit(solution)/shard_map/ppermute | solution.py:130
  58.5 2.3 %input_grad.1 = (f32[4,6,32,128]{3,2,1,0:T(8,128)S(1)}, f32[4,6,32,128]{3,2,1,0:T(8,128)S(1)}) custom-call(s32[4]{0:T(128)S(1)} %pad_add_fusion.where_ref, bf16[16,16,896]{2,1,0:T(8,128)(2,1)S(1)} %constant_dynamic-update-slice_fusion.own_ref, bf16[16,16,896]{2,1,0:T(8,128)(2,1)S(1)} %collective-permute-done.5.other_ref, ...), custom_call_target="tpu_custom_call" | custom-call | flops 1811939328 | bytes 8000000 | tf_op jit(solution)/shard_map/input_grad/pallas_call | solution.py:216
  60.8 2.1 %collective-permute-start.6 = (f32[4,6,32,128]{3,2,1,0:T(8,128)S(1)}, f32[4,6,32,128]{3,2,1,0:T(8,128)S(1)}, u32[]{:S(2)}, u32[]{:S(2)}) collective-permute-start(f32[4,6,32,128]{3,2,1,0:T(8,128)S(1)} %get-tuple-element.31), channel_id=1, source_target_pairs={{0,8},{8,0},{1,9},{9,1},{2,10},{10,2},{3,11},{11,3},{4,12},{12,4},... | collective-permute-start | bytes 1179656 | tf_op jit(solution)/shard_map/ppermute | solution.py:130
  63.0 0.0 collective-permute-done.12.recv_ref
  63.0 0.3 narrow.1
  63.2 0.8 convert_element_type.34
  64.1 7.7 %all-to-all-start.1 = ((f16[16,16,896]{2,1,0:T(8,128)(2,1)}), f16[16,16,896]{2,1,0:T(8,128)(2,1)S(1)}, u32[]{:S(2)}, u32[]{:S(2)}) async-start(f16[16,16,896]{2,1,0:T(8,128)(2,1)} %convert_element_type.34), calls=%async_computation.1 | async-start | bytes 917504 | tf_op jit(solution)/shard_map/all_to_all | solution.py:211
  71.8 1.2 %collective-permute-done.6 = f32[4,6,32,128]{3,2,1,0:T(8,128)S(1)} collective-permute-done((f32[4,6,32,128]{3,2,1,0:T(8,128)S(1)}, f32[4,6,32,128]{3,2,1,0:T(8,128)S(1)}, u32[]{:S(2)}, u32[]{:S(2)}) %collective-permute-start.6) | collective-permute-done | bytes 393248 | tf_op jit(solution)/shard_map/ppermute | solution.py:130
  73.0 0.1 add.30
  73.1 7.5 %collective-permute-start.7 = (f32[4,32,128]{2,1,0:T(8,128)S(1)}, f32[4,32,128]{2,1,0:T(8,128)S(1)}, u32[]{:S(2)}, u32[]{:S(2)}) collective-permute-start(f32[4,32,128]{2,1,0:T(8,128)S(1)} %get-tuple-element.41), channel_id=1, source_target_pairs={{0,16},{16,32},{32,48},{48,64},{64,80},{80,96},{96,112},{112,128},... | collective-permute-start | bytes 196616 | tf_op jit(solution)/shard_map/ppermute | solution.py:163
  80.7 1.9 %collective-permute-start.8 = (f32[4,32,128]{2,1,0:T(8,128)S(1)}, f32[4,32,128]{2,1,0:T(8,128)S(1)}, u32[]{:S(2)}, u32[]{:S(2)}) collective-permute-start(f32[4,32,128]{2,1,0:T(8,128)S(1)} %get-tuple-element.40), channel_id=1, source_target_pairs={{16,0},{32,16},{48,32},{64,48},{80,64},{96,80},{112,96},{128,112},... | collective-permute-start | bytes 196616 | tf_op jit(solution)/shard_map/ppermute | solution.py:168
  82.6 1.4 %collective-permute-done.7 = f32[4,32,128]{2,1,0:T(8,128)S(1)} collective-permute-done((f32[4,32,128]{2,1,0:T(8,128)S(1)}, f32[4,32,128]{2,1,0:T(8,128)S(1)}, u32[]{:S(2)}, u32[]{:S(2)}) %collective-permute-start.7) | collective-permute-done | bytes 65568 | tf_op jit(solution)/shard_map/ppermute | solution.py:163
  84.1 6.4 %collective-permute-done.8 = f32[4,32,128]{2,1,0:T(8,128)S(1)} collective-permute-done((f32[4,32,128]{2,1,0:T(8,128)S(1)}, f32[4,32,128]{2,1,0:T(8,128)S(1)}, u32[]{:S(2)}, u32[]{:S(2)}) %collective-permute-start.8) | collective-permute-done | bytes 65568 | tf_op jit(solution)/shard_map/ppermute | solution.py:168
  90.5 0.0 all-to-all-done.1
  90.5 0.1 convert_element_type.35
  90.6 0.2 fusion.4
  90.8 0.2 multiply_reduce_fusion
  90.9 1.9 %collective-permute-start.13 = (f32[16,896]{1,0:T(8,128)S(1)}, f32[16,896]{1,0:T(8,128)S(1)}, u32[]{:S(2)}, u32[]{:S(2)}) collective-permute-start(f32[16,896]{1,0:T(8,128)S(1)} %multiply_reduce_fusion), channel_id=1, source_target_pairs={{0,0},{8,256},{256,8},{264,264},{1,1},{9,257},{257,9},{265,265},{2... | collective-permute-start | bytes 172040 | tf_op jit(solution)/shard_map/ppermute | solution.py:134
  92.9 0.7 copy.22
  93.6 5.3 %collective-permute-done.13 = f32[16,896]{1,0:T(8,128)S(1)} collective-permute-done((f32[16,896]{1,0:T(8,128)S(1)}, f32[16,896]{1,0:T(8,128)S(1)}, u32[]{:S(2)}, u32[]{:S(2)}) %collective-permute-start.13) | collective-permute-done | bytes 57376 | tf_op jit(solution)/shard_map/ppermute | solution.py:134
  98.9 0.1 reshape.104
  99.0 0.8 copy.21
  (24 shorter events, 0.4 us)
Async XLA Ops:
  2.8 10.2 %copy-start.1 = (bf16[32,3,3,3,16]{0,4,3,2,1:T(8,128)(2,1)S(1)}, bf16[32,3,3,3,16]{0,4,3,2,1:T(8,128)(2,1)}, u32[]{:S(2)}) copy-start(bf16[32,3,3,3,16]{0,4,3,2,1:T(8,128)(2,1)} %param.11) | copy-start | bytes 82948
  2.8 45.6 %all-to-all-start = ((bf16[8,4,4,32,128]{4,3,2,1,0:T(8,128)(2,1)}), bf16[8,4,4,32,128]{4,3,2,1,0:T(8,128)(2,1)S(1)}, u32[]{:S(2)}, u32[]{:S(2)}) async-start(bf16[8,4,4,32,128]{4,3,2,1,0:T(8,128)(2,1)} %broadcast_in_dim.2), calls=%async_computation | async-start | bytes 2097152 | tf_op jit(solution)/shard_map/all_to_all | solution.py:182
  13.0 7.6 %copy-start = (s32[4,4,120,32]{2,3,1,0:T(8,128)S(1)}, s32[4,4,120,32]{2,3,1,0:T(8,128)}, u32[]{:S(2)}) copy-start(s32[4,4,120,32]{2,3,1,0:T(8,128)} %param.8) | copy-start | bytes 737284
  13.2 17.9 %collective-permute-start = (bf16[16,896]{1,0:T(8,128)(2,1)S(1)}, bf16[16,896]{1,0:T(8,128)(2,1)S(1)}, u32[]{:S(2)}, u32[]{:S(2)}) collective-permute-start(bf16[16,896]{1,0:T(8,128)(2,1)S(1)} %pad.15), channel_id=1, source_target_pairs={{0,0},{8,256},{256,8},{264,264},{1,1},{9,257},{257,9},{265,265},{2... | collective-permute-start | bytes 86024 | tf_op jit(solution)/shard_map/ppermute | solution.py:134
  17.8 13.2 %collective-permute-start.1 = (bf16[16,896]{1,0:T(8,128)(2,1)S(1)}, bf16[16,896]{1,0:T(8,128)(2,1)S(1)}, u32[]{:S(2)}, u32[]{:S(2)}) collective-permute-start(bf16[16,896]{1,0:T(8,128)(2,1)S(1)} %pad.15), channel_id=1, source_target_pairs={{0,256},{8,0},{256,264},{264,8},{1,257},{9,1},{257,265},{265,9},{2... | collective-permute-start | bytes 86024 | tf_op jit(solution)/shard_map/ppermute | solution.py:138
  20.7 18.5 %collective-permute-start.10 = (bf16[4,1,32,128]{3,2,1,0:T(8,128)(2,1)S(1)}, bf16[4,1,32,128]{3,2,1,0:T(8,128)(2,1)S(1)}, u32[]{:S(2)}, u32[]{:S(2)}) collective-permute-start(bf16[4,1,32,128]{3,2,1,0:T(8,128)(2,1)S(1)} %get-tuple-element.43), channel_id=1, source_target_pairs={{16,0},{32,16},{48,32},{64,48},{80,64},{96,80},{112,96},{128,112},... | collective-permute-start | bytes 98312 | tf_op jit(solution)/shard_map/ppermute | solution.py:168
  23.8 15.4 %collective-permute-start.9 = (bf16[4,1,32,128]{3,2,1,0:T(8,128)(2,1)S(1)}, bf16[4,1,32,128]{3,2,1,0:T(8,128)(2,1)S(1)}, u32[]{:S(2)}, u32[]{:S(2)}) collective-permute-start(bf16[4,1,32,128]{3,2,1,0:T(8,128)(2,1)S(1)} %get-tuple-element.42), channel_id=1, source_target_pairs={{0,16},{16,32},{32,48},{48,64},{64,80},{80,96},{96,112},{112,128},... | collective-permute-start | bytes 98312 | tf_op jit(solution)/shard_map/ppermute | solution.py:163
  31.1 6.1 %collective-permute-start.2 = (bf16[2,16,896]{2,1,0:T(8,128)(2,1)S(1)}, bf16[2,16,896]{2,1,0:T(8,128)(2,1)S(1)}, u32[]{:S(2)}, u32[]{:S(2)}) collective-permute-start(bf16[2,16,896]{2,1,0:T(8,128)(2,1)S(1)} %pad_maximum_fusion.3), channel_id=1, source_target_pairs={{0,128},{32,160},{64,192},{96,224},{128,0},{160,32},{192,64},{224,... | collective-permute-start | bytes 172040 | tf_op jit(solution)/shard_map/ppermute | solution.py:156
  37.2 7.9 %collective-permute-start.3 = (bf16[4,16,896]{2,1,0:T(8,128)(2,1)S(1)}, bf16[4,16,896]{2,1,0:T(8,128)(2,1)S(1)}, u32[]{:S(2)}, u32[]{:S(2)}) collective-permute-start(bf16[4,16,896]{2,1,0:T(8,128)(2,1)S(1)} %pad_maximum_fusion.2), channel_id=1, source_target_pairs={{0,64},{32,96},{64,0},{96,32},{128,192},{160,224},{192,128},{224,1... | collective-permute-start | bytes 344072 | tf_op jit(solution)/shard_map/ppermute | solution.py:156
  39.2 9.1 %collective-permute-start.11 = (bf16[4,6,32,128]{3,2,1,0:T(8,128)(2,1)S(1)}, bf16[4,6,32,128]{3,2,1,0:T(8,128)(2,1)S(1)}, u32[]{:S(2)}, u32[]{:S(2)}) collective-permute-start(bf16[4,6,32,128]{3,2,1,0:T(8,128)(2,1)S(1)} %pad_maximum_fusion.1.own_ref), channel_id=1, source_target_pairs={{0,8},{8,0},{1,9},{9,1},{2,10},{10,2},{3,11},{11,3},{4,12},{12,4},... | collective-permute-start | bytes 589832 | tf_op jit(solution)/shard_map/ppermute | solution.py:130
  45.2 9.5 %collective-permute-start.4 = (bf16[8,16,896]{2,1,0:T(8,128)(2,1)S(1)}, bf16[8,16,896]{2,1,0:T(8,128)(2,1)S(1)}, u32[]{:S(2)}, u32[]{:S(2)}) collective-permute-start(bf16[8,16,896]{2,1,0:T(8,128)(2,1)S(1)} %pad_maximum_fusion), channel_id=1, source_target_pairs={{0,32},{32,0},{64,96},{96,64},{128,160},{160,128},{192,224},{224,1... | collective-permute-start | bytes 688136 | tf_op jit(solution)/shard_map/ppermute | solution.py:156
  51.8 11.2 %collective-permute-start.12 = (f32[2,8,16,896]{3,2,1,0:T(8,128)S(1)}, f32[2,8,16,896]{3,2,1,0:T(8,128)S(1)}, u32[]{:S(2)}, u32[]{:S(2)}) collective-permute-start(f32[2,8,16,896]{3,2,1,0:T(8,128)S(1)} %get-tuple-element.33), channel_id=1, source_target_pairs={{0,16},{16,0},{1,17},{17,1},{2,18},{18,2},{3,19},{19,3},{4,20},{20... | collective-permute-start | bytes 2752520 | tf_op jit(solution)/shard_map/ppermute | solution.py:130
  54.8 3.7 %collective-permute-start.5 = (bf16[16,16,896]{2,1,0:T(8,128)(2,1)S(1)}, bf16[16,16,896]{2,1,0:T(8,128)(2,1)S(1)}, u32[]{:S(2)}, u32[]{:S(2)}) collective-permute-start(bf16[16,16,896]{2,1,0:T(8,128)(2,1)S(1)} %constant_dynamic-update-slice_fusion.own_ref), channel_id=1, source_target_pairs={{0,16},{16,0},{1,17},{17,1},{2,18},{18,2},{3,19},{19,3},{4,20},{20... | collective-permute-start | bytes 1376264 | tf_op jit(solution)/shard_map/ppermute | solution.py:130
  60.8 12.2 %collective-permute-start.6 = (f32[4,6,32,128]{3,2,1,0:T(8,128)S(1)}, f32[4,6,32,128]{3,2,1,0:T(8,128)S(1)}, u32[]{:S(2)}, u32[]{:S(2)}) collective-permute-start(f32[4,6,32,128]{3,2,1,0:T(8,128)S(1)} %get-tuple-element.31), channel_id=1, source_target_pairs={{0,8},{8,0},{1,9},{9,1},{2,10},{10,2},{3,11},{11,3},{4,12},{12,4},... | collective-permute-start | bytes 1179656 | tf_op jit(solution)/shard_map/ppermute | solution.py:130
  64.1 26.4 %all-to-all-start.1 = ((f16[16,16,896]{2,1,0:T(8,128)(2,1)}), f16[16,16,896]{2,1,0:T(8,128)(2,1)S(1)}, u32[]{:S(2)}, u32[]{:S(2)}) async-start(f16[16,16,896]{2,1,0:T(8,128)(2,1)} %convert_element_type.34), calls=%async_computation.1 | async-start | bytes 917504 | tf_op jit(solution)/shard_map/all_to_all | solution.py:211
  73.1 10.9 %collective-permute-start.7 = (f32[4,32,128]{2,1,0:T(8,128)S(1)}, f32[4,32,128]{2,1,0:T(8,128)S(1)}, u32[]{:S(2)}, u32[]{:S(2)}) collective-permute-start(f32[4,32,128]{2,1,0:T(8,128)S(1)} %get-tuple-element.41), channel_id=1, source_target_pairs={{0,16},{16,32},{32,48},{48,64},{64,80},{80,96},{96,112},{112,128},... | collective-permute-start | bytes 196616 | tf_op jit(solution)/shard_map/ppermute | solution.py:163
  80.7 9.8 %collective-permute-start.8 = (f32[4,32,128]{2,1,0:T(8,128)S(1)}, f32[4,32,128]{2,1,0:T(8,128)S(1)}, u32[]{:S(2)}, u32[]{:S(2)}) collective-permute-start(f32[4,32,128]{2,1,0:T(8,128)S(1)} %get-tuple-element.40), channel_id=1, source_target_pairs={{16,0},{32,16},{48,32},{64,48},{80,64},{96,80},{112,96},{128,112},... | collective-permute-start | bytes 196616 | tf_op jit(solution)/shard_map/ppermute | solution.py:168
  90.9 7.9 %collective-permute-start.13 = (f32[16,896]{1,0:T(8,128)S(1)}, f32[16,896]{1,0:T(8,128)S(1)}, u32[]{:S(2)}, u32[]{:S(2)}) collective-permute-start(f32[16,896]{1,0:T(8,128)S(1)} %multiply_reduce_fusion), channel_id=1, source_target_pairs={{0,0},{8,256},{256,8},{264,264},{1,1},{9,257},{257,9},{265,265},{2... | collective-permute-start | bytes 172040 | tf_op jit(solution)/shard_map/ppermute | solution.py:134
